TPU v7x, 512 devices: a whole 4x4x16 slice. The times are simulated.
512 devices in a mesh: blk: 64 (over x, z), span: 8 (over y, core).
Axes of the slice: x: 4, y: 4, z: 16, core: 2. Of those that a mesh axis runs over, the one named last changes fastest.
Arguments:
- fields: float32 [5, 6, 6, 6, 131072], P(None, None, None, None, ('blk', 'span')), may hold values from -6 to 6
- jacobian: float32 [131072], P(('blk', 'span')), may hold values from 0.5 to 2
- mean_flow: float32 [3], replicated, may hold values from -0.5 to 0.5
- pair_owner: int32 [65536, 1], P(('blk', 'span')), may hold values from 0 to 63, as said below
- pair_mortar: int32 [65536], P(('blk', 'span')), may hold values from 0 to 63
- mortar_proj: float32 [2, 2, 6, 6], replicated, may hold values from -2.5 to 2.5
- coarse_id: int32 [131072], P(('blk', 'span')), may hold values from 0 to 255
Outputs:
- new_fields: float32 [5, 6, 6, 6, 131072], P(None, None, None, None, ('blk', 'span'))
- coarse_residual: float32 [40, 16384], P(None, ('blk', 'span'))
Inputs may be any that keep to these rules, and one draw needn't show every extreme that they name: `pair_owner`: the owner of every pair of a device with blk index b is b - 1, b or b + 1 modulo 64; among the 128 pairs of one device at most 64 name the same owner, and in every draw some owner is named by exactly 64 of them.
All inputs are finite; a program needn't handle non-finite values.
Results may differ from a plain program's by a relative error of at most 0.0003.
Values sent between devices are 32-bit elements; how exact they have to be, the bound alone decides.
No kernel may reach another device: no remote copies, remote signals or barrier semaphores. Data moves between devices by JAX's collectives and lax.ppermute only.
A program may use at most 128 MiB of HBM per device.

v0:
```python
import jax
import jax.numpy as jnp
import numpy as np
from jax import lax
from jax.sharding import PartitionSpec as P

NP = 6
NV = 5


time_step = 0.02
lift_scale = 15.0


def shifted(value, axis, steps):
    count = lax.axis_size(axis)
    pairs = [(source, (source + steps) % count) for source in range(count)]
    return lax.ppermute(value, axis, pairs)


def node_table():
    return np.array(
        [
            -1.0,
            -0.7650553239294647,
            -0.2852315164806451,
            0.2852315164806451,
            0.7650553239294647,
            1.0,
        ]
    )


def weight_table():
    return np.array(
        [
            1.0 / 15.0,
            0.378474956297847,
            0.5548583770354863,
            0.5548583770354863,
            0.378474956297847,
            1.0 / 15.0,
        ]
    )


def derivative_table():
    nodes = node_table()
    count = nodes.shape[0]
    barycentric = np.ones(count)
    for first in range(count):
        for other in range(count):
            if other != first:
                barycentric[first] = barycentric[first] / (nodes[first] - nodes[other])
    table = np.zeros((count, count))
    for row_index in range(count):
        for col_index in range(count):
            if row_index != col_index:
                table[row_index, col_index] = (
                    barycentric[col_index]
                    / barycentric[row_index]
                    / (nodes[row_index] - nodes[col_index])
                )
        table[row_index, row_index] = -np.sum(table[row_index])
    return table


def coarse_table():
    return np.stack([weight_table(), weight_table() * node_table()])


def volume_term(fields, jacobian, mean_flow):
    deriv_table = jnp.asarray(derivative_table(), jnp.float32)
    grad_x = jnp.einsum("ai,vijke->vajke", deriv_table, fields, precision=lax.Precision.HIGHEST)
    grad_y = jnp.einsum("bj,vijke->vibke", deriv_table, fields, precision=lax.Precision.HIGHEST)
    grad_z = jnp.einsum("ck,vijke->vijce", deriv_table, fields, precision=lax.Precision.HIGHEST)
    advect = mean_flow[0] * grad_x + mean_flow[1] * grad_y + mean_flow[2] * grad_z
    spread = grad_x[1] + grad_y[2] + grad_z[3]
    result = jnp.stack(
        [
            advect[0] + spread,
            advect[1] + grad_x[4],
            advect[2] + grad_y[4],
            advect[3] + grad_z[4],
            advect[4] + spread,
        ]
    )
    return -jacobian * result


def normal_flux(trace, axial_flow):
    return jnp.stack(
        [
            axial_flow * trace[0] + trace[3],
            axial_flow * trace[1],
            axial_flow * trace[2],
            axial_flow * trace[3] + trace[4],
            axial_flow * trace[4] + trace[3],
        ]
    )


def riemann(inner, outer, axial_flow):
    return 0.5 * (normal_flux(inner, axial_flow) + normal_flux(outer, axial_flow)) - 0.5 * (
        jnp.abs(axial_flow) + 1.0
    ) * (outer - inner)


def project(side_mats, upper, trace):
    lower_part = jnp.einsum("ai,vijs->vajs", side_mats[0], trace, precision=lax.Precision.HIGHEST)
    upper_part = jnp.einsum("ai,vijs->vajs", side_mats[1], trace, precision=lax.Precision.HIGHEST)
    return jnp.where(upper, upper_part, lower_part)


def back_project(side_mats, upper, trace):
    lower_part = jnp.einsum("ia,vajs->vijs", side_mats[0], trace, precision=lax.Precision.HIGHEST)
    upper_part = jnp.einsum("ia,vajs->vijs", side_mats[1], trace, precision=lax.Precision.HIGHEST)
    return jnp.where(upper, upper_part, lower_part)


def coarse_partial(field, jacobian, coarse_id, agg_count):
    weights = jnp.asarray(coarse_table(), jnp.float32)
    first = jnp.einsum("ai,vijke->vajke", weights, field, precision=lax.Precision.HIGHEST)
    second = jnp.einsum("bj,vajke->vabke", weights, first, precision=lax.Precision.HIGHEST)
    third = jnp.einsum("ck,vabke->vabce", weights, second, precision=lax.Precision.HIGHEST)
    scaled = (third / (jacobian * jacobian * jacobian)).reshape(NV * 8, field.shape[4])
    member = (coarse_id[:, None] == jnp.arange(agg_count, dtype=jnp.int32)[None, :]).astype(
        jnp.float32
    )
    return jnp.dot(scaled, member, precision=lax.Precision.HIGHEST)


def rank_slots(key_row, key_count, capacity):
    key_hot = (key_row[:, None] == jnp.arange(key_count, dtype=jnp.int32)[None, :]).astype(
        jnp.int32
    )
    before = jnp.cumsum(key_hot, axis=0) - key_hot
    slot_rank = jnp.sum(before * key_hot, axis=1)
    slot_index = key_row * capacity + slot_rank
    return (
        slot_index[:, None] == jnp.arange(key_count * capacity, dtype=jnp.int32)[None, :]
    ).astype(jnp.float32)


def residual(fields, jacobian, mean_flow, owner_row, mortar_row, matrices):
    face_count = fields.shape[4] // 4
    pair_count = 2 * face_count
    capacity = pair_count // 2
    sectors = lax.axis_size("blk")
    here = lax.axis_index("blk")
    axial_flow = mean_flow[2]
    rotor_trace = fields[:, :, :, 5, :face_count]
    stator_trace = fields[:, :, :, 0, face_count : 2 * face_count]
    pair_trace = jnp.repeat(rotor_trace, 2, axis=3)
    half_pair = jnp.arange(pair_count, dtype=jnp.int32) % 2
    face_nodes = NV * NP * NP
    relative = (owner_row - here + sectors) % sectors
    lane = jnp.where(relative == sectors - 1, 0, jnp.where(relative == 0, 1, 2)).astype(jnp.int32)
    select = rank_slots(lane, 3, capacity)
    labels = jnp.stack([mortar_row + 1, half_pair]).astype(jnp.float32)
    rows = jnp.concatenate([pair_trace.reshape(face_nodes, pair_count), labels], axis=0)
    packed = jnp.dot(rows, select, precision=lax.Precision.HIGHEST)
    pieces = []
    for lane_pos, delta in enumerate((-1, 0, 1)):
        block = packed[:, lane_pos * capacity : (lane_pos + 1) * capacity]
        if delta != 0:
            block = shifted(block, "blk", delta)
        pieces.append(block)
    arrived_rows = jnp.concatenate(pieces, axis=1)
    slot_count = 3 * capacity
    arrived = arrived_rows[:face_nodes]
    mortar_label = arrived_rows[face_nodes].astype(jnp.int32) - 1
    offset_hot = (mortar_label[None, :] == jnp.arange(face_count, dtype=jnp.int32)[:, None]).astype(
        jnp.float32
    )
    stator_slot = jnp.dot(
        stator_trace.reshape(face_nodes, face_count), offset_hot, precision=lax.Precision.HIGHEST
    )
    upper = arrived_rows[face_nodes + 1] > 0.5
    mortar_flux = riemann(
        project(matrices[0], upper, arrived.reshape(NV, NP, NP, slot_count)),
        project(matrices[1], upper, stator_slot.reshape(NV, NP, NP, slot_count)),
        axial_flow,
    )
    outgoing = back_project(matrices[0], upper, mortar_flux).reshape(face_nodes, slot_count)
    backs = []
    for lane_pos, delta in enumerate((-1, 0, 1)):
        block = outgoing[:, lane_pos * capacity : (lane_pos + 1) * capacity]
        if delta != 0:
            block = shifted(block, "blk", -delta)
        backs.append(block)
    returned = jnp.concatenate(backs, axis=1)
    pair_flux = jnp.dot(returned, select.T, precision=lax.Precision.HIGHEST)
    stator_terms = back_project(matrices[1], upper, mortar_flux).reshape(face_nodes, slot_count)
    stator_sum = jnp.dot(stator_terms, offset_hot.T, precision=lax.Precision.HIGHEST)
    rotor_sum = pair_flux.reshape(NV, NP, NP, face_count, 2).sum(axis=4)
    rotor_lift = (
        lift_scale * jacobian[:face_count] * (normal_flux(rotor_trace, axial_flow) - rotor_sum)
    )
    stator_lift = (
        lift_scale
        * jacobian[face_count : 2 * face_count]
        * (stator_sum.reshape(NV, NP, NP, face_count) - normal_flux(stator_trace, axial_flow))
    )
    volume = volume_term(fields, jacobian, mean_flow)
    volume = volume.at[:, :, :, 5, :face_count].add(rotor_lift)
    volume = volume.at[:, :, :, 0, face_count : 2 * face_count].add(stator_lift)
    return volume


def local(fields, jacobian, mean_flow, pair_owner, pair_mortar, mortar_proj, coarse_id):
    owner_row = pair_owner[:, 0]
    spans = lax.axis_size("span")
    agg_count = fields.shape[4] * spans // 8
    first_rate = residual(fields, jacobian, mean_flow, owner_row, pair_mortar, mortar_proj)
    section_one = fields + time_step * first_rate
    second_rate = residual(section_one, jacobian, mean_flow, owner_row, pair_mortar, mortar_proj)
    new_fields = 0.5 * fields + 0.5 * (section_one + time_step * second_rate)
    coarse_residual = jnp.zeros((NV * 8, agg_count // spans), jnp.float32)
    for section_rate in (first_rate, second_rate):
        partial_sums = 0.5 * coarse_partial(section_rate, jacobian, coarse_id, agg_count)
        coarse_residual = coarse_residual + lax.psum_scatter(
            partial_sums, "span", scatter_dimension=1, tiled=True
        )
    return (new_fields, coarse_residual)


def solution(mesh):
    return jax.shard_map(
        local,
        mesh=mesh,
        in_specs=(
            P(None, None, None, None, ("blk", "span")),
            P(("blk", "span")),
            P(),
            P(("blk", "span"), None),
            P(("blk", "span")),
            P(),
            P(("blk", "span")),
        ),
        out_specs=(P(None, None, None, None, ("blk", "span")), P(None, ("blk", "span"))),
        check_vma=False,
    )
```

profile of v0, /device:TPU:1, one launch (start us, length us, event | category | flops | bytes accessed | tf_op | source)
XLA Modules:
  0.0 221.4 jit_solution(9405655504597243218)
XLA Ops:
  9.0 1.7 fusion.116
  11.3 1.7 broadcast_in_dim.28
  13.0 2.4 %reshape_reshape.6 = f32[180,128]{0,1:T(8,128)S(1)} reshape(f32[5,6,6,64,2]{2,1,0,4,3:T(8,128)} %broadcast_in_dim.28) | data formatting | bytes 184320 | tf_op jit(solution)/shard_map/reshape;reshape | solution.py:161
  15.9 14.1 %collective-permute-start = (f32[182,64]{1,0:T(8,128)S(1)}, f32[182,64]{1,0:T(8,128)S(1)}, u32[]{:S(2)}, u32[]{:S(2)}) collective-permute-start(f32[182,64]{1,0:T(8,128)S(1)} %get-tuple-element.84), channel_id=1, source_target_pairs={{0,504},{8,0},{16,8},{24,16},{32,24},{40,32},{48,40},{56,48},{64,5... | collective-permute-start | bytes 139784 | tf_op jit(solution)/shard_map/ppermute | solution.py:18
  30.1 2.4 %collective-permute-start.1 = (f32[182,64]{1,0:T(8,128)S(1)}, f32[182,64]{1,0:T(8,128)S(1)}, u32[]{:S(2)}, u32[]{:S(2)}) collective-permute-start(f32[182,64]{1,0:T(8,128)S(1)} %get-tuple-element.85), channel_id=1, source_target_pairs={{0,8},{8,16},{16,24},{24,32},{32,40},{40,48},{48,56},{56,64},{64,7... | collective-permute-start | bytes 139784 | tf_op jit(solution)/shard_map/ppermute | solution.py:18
  32.6 1.9 convolution_bitcast_fusion.1
  34.5 1.3 fusion.125
  35.9 1.6 fusion.4
  40.8 3.3 %fusion.117 = (f32[5,6,6,6,256]{4,1,2,3,0:T(8,128)S(1)}, f32[5,6,6,6,256]{4,1,2,3,0:T(8,128)S(1)}) fusion(f32[5,6,6,6,256]{4,1,3,2,0:T(8,128)S(1)} %convolution_bitcast_fusion.1, f32[6,5,6,6,256]{4,0,3,2,1:T(8,128)S(1)} %fusion.125, f32[]{:T(128)} %bitcast.7, f32[6,5,6,6,256]{4,0,3,2,1:T(8,128)S(1)} %fusion.4, f32[]{:T(128)} %bitcast.4, f32[]{:T(128)} %bitcast), kind=kLoop, calls=%fused_computation.276 | loop fusion | flops 1382400 | bytes 5529612 | tf_op jit(solution)/shard_map/ai,vijke->vajke/transpose | solution.py:74
  50.8 1.2 broadcast_multiply_fusion
  63.1 1.9 collective-permute-start.2
  65.0 6.9 %collective-permute-start.3 = (f32[180,64]{1,0:T(8,128)S(1)}, f32[180,64]{1,0:T(8,128)S(1)}, u32[]{:S(2)}, u32[]{:S(2)}) collective-permute-start(f32[180,64]{1,0:T(8,128)S(1)} %get-tuple-element.82), channel_id=1, source_target_pairs={{0,504},{8,0},{16,8},{24,16},{32,24},{40,32},{48,40},{56,48},{64,5... | collective-permute-start | bytes 138248 | tf_op jit(solution)/shard_map/ppermute | solution.py:18
  72.3 1.1 collective-permute-done.3
  73.7 2.1 reshape.672
  75.8 2.2 reduce_sum.39
  78.4 0.9 fusion.67
  79.4 1.7 scatter-add.14
  81.1 3.2 %fusion.22 = f32[5,6,6,1,64]{4,1,3,2,0:T(8,128)S(1)} fusion(f32[5,6,6,64]{3,1,2,0:T(8,128)S(1)} %constant_dynamic-update-slice_fusion.15, f32[5,6,6,192]{3,1,2,0:T(8,128)S(1)} %fusion.11, f32[5,6,6,6,256]{4,1,3,2,0:T(8,128)} %scatter-add.14, s32[]{:T(128)} %bitcast.35, s32[]{:T(128)} %bitcast.36, f32[64]{0:T(128)S(1)} %get-tuple-element.93, ...), kind=kOutput, calls=%fused_computation.48 | convolution fusion | flops 26600448 | bytes 277513 | tf_op jit(solution)/shard_map/dot_general | solution.py:195
  84.3 7.2 %scatter-add.15 = f32[5,6,6,6,256]{4,1,3,2,0:T(8,128)} dynamic-update-slice(f32[5,6,6,6,256]{4,1,3,2,0:T(8,128)} %scatter-add.14, f32[5,6,6,1,64]{4,1,3,2,0:T(8,128)S(1)} %fusion.22, s32[]{:T(128)} %constant.157.clone.1, s32[]{:T(128)} %constant.157.clone.1, s32[]{:T(128)} %constant.157.clone.1, s32[]{:T(128)} %bitcast.35, s32[]{:T(128)} %bitcast.36) | dynamic-update-slice | bytes 92164 | tf_op jit(solution)/shard_map/scatter-add | solution.py:207
  91.4 2.2 multiply_add_fusion.1
  95.0 2.8 %fusion = f32[5,6,6,256,6]{3,4,2,1,0:T(8,128)} fusion(f32[6,6,1,1,1]{1,0,4,3,2:T(8,128)S(1)} %copy-done.5, f32[5,6,6,6,256]{4,1,3,2,0:T(8,128)S(1)} %multiply_add_fusion.1), kind=kOutput, calls=%fused_computation.1 | convolution fusion | flops 19906560 | bytes 2211984 | tf_op jit(solution)/shard_map/ck,vijke->vijce/dot_general | solution.py:76
  97.8 3.2 %fusion.2 = f32[5,6,6,256,6]{3,4,2,1,0:T(8,128)} fusion(f32[6,6,1,1,1]{1,0,4,3,2:T(8,128)S(1)} %copy-done.5, f32[5,6,6,6,256]{4,1,3,2,0:T(8,128)S(1)} %multiply_add_fusion.1), kind=kOutput, calls=%fused_computation.4 | convolution fusion | flops 19906560 | bytes 2211984 | tf_op jit(solution)/shard_map/bj,vijke->vibke/dot_general | solution.py:75
  100.9 1.6 copy.203
  102.5 3.0 %broadcast_in_dim.31 = f32[5,6,6,64,2]{2,1,0,4,3:T(8,128)} broadcast(f32[5,6,6,64]{2,1,0,3:T(8,128)} %copy.203), dimensions={0,1,2,3} | broadcast | bytes 138240 | tf_op jit(solution)/shard_map/broadcast_in_dim | solution.py:154
  105.4 2.3 %reshape_reshape.7 = f32[180,128]{0,1:T(8,128)S(1)} reshape(f32[5,6,6,64,2]{2,1,0,4,3:T(8,128)} %broadcast_in_dim.31) | data formatting | bytes 184320 | tf_op jit(solution)/shard_map/reshape;reshape | solution.py:161
  108.8 7.0 %collective-permute-start.4 = (f32[182,64]{1,0:T(8,128)}, f32[182,64]{1,0:T(8,128)S(1)}, u32[]{:S(2)}, u32[]{:S(2)}) collective-permute-start(f32[182,64]{1,0:T(8,128)} %get-tuple-element.78), channel_id=1, source_target_pairs={{0,504},{8,0},{16,8},{24,16},{32,24},{40,32},{48,40},{56,48},{64,5... | collective-permute-start | bytes 139784 | tf_op jit(solution)/shard_map/ppermute | solution.py:18
  115.8 2.1 collective-permute-start.5
  122.6 2.1 copy.425
  126.1 4.4 %multiply_add_fusion = (f32[5,6,6,6,256]{4,1,2,3,0:T(8,128)S(1)}, f32[5,6,6,6,256]{4,1,2,3,0:T(8,128)S(1)}) fusion(f32[]{:T(128)} %bitcast.7, f32[]{:T(128)} %bitcast.4, f32[]{:T(128)} %bitcast, f32[5,6,6,256,6]{3,4,2,1,0:T(8,128)S(1)} %copy-done.2, f32[5,6,6,256,6]{3,4,2,1,0:T(8,128)S(1)} %copy-done.1, f32[6,6,1,1,1]{1,0,3,4,2:T(8,128)S(1)} %copy-done.11, ...), kind=kOutput, calls=%fused_computation.11 | convolution fusion | flops 21288960 | bytes 5529756 | tf_op jit(solution)/shard_map/ai,vijke->vajke/dot_general | solution.py:74
  130.8 1.3 broadcast_multiply_fusion.1
  132.1 2.8 %convolution_bitcast_fusion.3 = f32[5,2,6,6,256]{4,1,3,2,0:T(2,128)S(1)} fusion(f32[5,6,6,6,256]{4,1,3,2,0:T(8,128)} %scatter-add.15, f32[2,6,1,1,1]{1,0,4,3,2:T(2,128)S(1)} %copy-done.6), kind=kOutput, calls=%fused_computation.18 | convolution fusion | flops 6635520 | bytes 1474608 | tf_op jit(solution)/shard_map/ai,vijke->vajke/dot_general | solution.py:123
  135.5 0.9 fusion.26
  137.2 1.1 fusion.35
  148.6 1.9 collective-permute-start.6
  150.5 6.9 %collective-permute-start.7 = (f32[180,64]{1,0:T(8,128)S(1)}, f32[180,64]{1,0:T(8,128)S(1)}, u32[]{:S(2)}, u32[]{:S(2)}) collective-permute-start(f32[180,64]{1,0:T(8,128)S(1)} %get-tuple-element.76), channel_id=1, source_target_pairs={{0,504},{8,0},{16,8},{24,16},{32,24},{40,32},{48,40},{56,48},{64,5... | collective-permute-start | bytes 138248 | tf_op jit(solution)/shard_map/ppermute | solution.py:18
  157.8 1.0 collective-permute-done.7
  159.1 2.1 reshape.678
  161.3 2.2 reduce_sum.41
  163.9 0.9 slice_add_fusion.14
  164.9 1.8 scatter-add.16
  166.6 1.6 copy.221
  168.2 3.2 %fusion.24 = f32[5,6,6,1,64]{4,1,3,2,0:T(8,128)S(1)} fusion(f32[5,6,6,64]{3,1,2,0:T(8,128)S(1)} %copy-done.4, f32[5,6,6,192]{3,1,2,0:T(8,128)S(1)} %fusion.7, s32[]{:T(128)} %bitcast.35, s32[]{:T(128)} %bitcast.36, f32[64]{0:T(128)S(1)} %get-tuple-element.93, pred[]{:T(512)} %and_reduce_fusion, s32[192]{0:T(256)S(1)} %bitcast.293, ...), kind=kOutput, calls=%fused_computation.50 | convolution fusion | flops 26600448 | bytes 355840 | tf_op jit(solution)/shard_map/dot_general | solution.py:195
  171.4 5.9 %scatter-add.19 = f32[5,6,6,6,256]{4,1,3,2,0:T(8,128)S(1)} dynamic-update-slice(f32[5,6,6,6,256]{4,1,3,2,0:T(8,128)S(1)} %copy.221, f32[5,6,6,1,64]{4,1,3,2,0:T(8,128)S(1)} %fusion.24, s32[]{:T(128)} %constant.157.clone.1, s32[]{:T(128)} %constant.157.clone.1, s32[]{:T(128)} %constant.157.clone.1, s32[]{:T(128)} %bitcast.35, s32[]{:T(128)} %bitcast.36) | dynamic-update-slice | bytes 92164 | tf_op jit(solution)/shard_map/scatter-add | solution.py:207
  177.3 1.4 convolution_bitcast_fusion.2
  179.6 1.1 fusion.15
  180.8 2.4 %add_multiply_fusion = f32[5,6,6,6,256]{4,1,3,2,0:T(8,128)S(1)} fusion(f32[5,6,6,6,256]{4,1,3,2,0:T(8,128)S(1)} %scatter-add.19, f32[5,6,6,6,256]{4,3,2,1,0:T(8,128)S(1)} %copy-done, f32[5,6,6,6,256]{4,1,3,2,0:T(8,128)} %scatter-add.15), kind=kLoop, calls=%fused_computation.10 | loop fusion | flops 1658880 | bytes 4423680 | tf_op jit(solution)/shard_map/add | solution.py:218
  183.2 1.5 copy.227
  184.6 29.7 %reduce-scatter.2.cloned.1.call-done = f32[40,32]{0,1:T(8,128)} async-done(((f32[40,256]{0,1:T(8,128)}), f32[40,32]{0,1:T(8,128)}) %reduce-scatter.2.cloned.1.call-update) | async-done | bytes 5136 | tf_op jit(solution)/shard_map/reduce_scatter | solution.py:222
  (166 shorter events, 46.3 us)
Async XLA Ops:
  7.2 207.2 %reduce-scatter.2.cloned.1.call-start = ((), (), s32[]{:S(2)}) async-start(), calls=%async_computation.1 | async-start | bytes 147456 | tf_op jit(solution)/shard_map/reduce_scatter | solution.py:222
  13.0 2.4 %copy-start.17 = (s32[128]{0:T(128)S(1)}, s32[128]{0:T(128)}, u32[]{:S(2)}) copy-start(s32[128]{0:T(128)} %param.23) | copy-start | bytes 1540
  13.0 19.6 %copy-start = (f32[5,6,6,6,256]{4,3,2,1,0:T(8,128)S(1)}, f32[5,6,6,6,256]{4,3,2,1,0:T(8,128)}, u32[]{:S(2)}) copy-start(f32[5,6,6,6,256]{4,3,2,1,0:T(8,128)} %param.19) | copy-start | bytes 3317764
  13.0 19.6 %copy-start.5 = (f32[6,6,1,1,1]{1,0,4,3,2:T(8,128)S(1)}, f32[6,6,1,1,1]{1,0,4,3,2:T(8,128)}, u32[]{:S(2)}) copy-start(f32[6,6,1,1,1]{1,0,4,3,2:T(8,128)} %constant.179) | copy-start | bytes 436
  15.9 38.1 %collective-permute-start = (f32[182,64]{1,0:T(8,128)S(1)}, f32[182,64]{1,0:T(8,128)S(1)}, u32[]{:S(2)}, u32[]{:S(2)}) collective-permute-start(f32[182,64]{1,0:T(8,128)S(1)} %get-tuple-element.84), channel_id=1, source_target_pairs={{0,504},{8,0},{16,8},{24,16},{32,24},{40,32},{48,40},{56,48},{64,5... | collective-permute-start | bytes 139784 | tf_op jit(solution)/shard_map/ppermute | solution.py:18
  30.1 23.9 %collective-permute-start.1 = (f32[182,64]{1,0:T(8,128)S(1)}, f32[182,64]{1,0:T(8,128)S(1)}, u32[]{:S(2)}, u32[]{:S(2)}) collective-permute-start(f32[182,64]{1,0:T(8,128)S(1)} %get-tuple-element.85), channel_id=1, source_target_pairs={{0,8},{8,16},{16,24},{24,32},{32,40},{40,48},{48,56},{56,64},{64,7... | collective-permute-start | bytes 139784 | tf_op jit(solution)/shard_map/ppermute | solution.py:18
  35.8 1.9 copy-start.13
  35.9 3.0 %copy-start.7 = (f32[2,2,6,6]{3,1,2,0:T(2,128)S(1)}, f32[2,2,6,6]{3,1,2,0:T(2,128)}, u32[]{:S(2)}) copy-start(f32[2,2,6,6]{3,1,2,0:T(2,128)} %param.24) | copy-start | bytes 1732
  35.9 3.0 %copy-start.10 = (f32[3]{0:T(128)S(1)}, f32[3]{0:T(128)}, u32[]{:S(2)}) copy-start(f32[3]{0:T(128)} %param.21) | copy-start | bytes 40
  50.7 1.3 copy-start.16
  63.1 9.1 %collective-permute-start.2 = (f32[180,64]{1,0:T(8,128)S(1)}, f32[180,64]{1,0:T(8,128)S(1)}, u32[]{:S(2)}, u32[]{:S(2)}) collective-permute-start(f32[180,64]{1,0:T(8,128)S(1)} %get-tuple-element.81), channel_id=1, source_target_pairs={{0,8},{8,16},{16,24},{24,32},{32,40},{40,48},{48,56},{56,64},{64,7... | collective-permute-start | bytes 138248 | tf_op jit(solution)/shard_map/ppermute | solution.py:18
  65.0 8.3 %collective-permute-start.3 = (f32[180,64]{1,0:T(8,128)S(1)}, f32[180,64]{1,0:T(8,128)S(1)}, u32[]{:S(2)}, u32[]{:S(2)}) collective-permute-start(f32[180,64]{1,0:T(8,128)S(1)} %get-tuple-element.82), channel_id=1, source_target_pairs={{0,504},{8,0},{16,8},{24,16},{32,24},{40,32},{48,40},{56,48},{64,5... | collective-permute-start | bytes 138248 | tf_op jit(solution)/shard_map/ppermute | solution.py:18
  75.8 2.7 %copy-start.8 = (f32[64]{0:T(128)S(1)}, f32[64]{0:T(128)}, u32[]{:S(2)}) copy-start(f32[64]{0:T(128)} %get-tuple-element.94) | copy-start | bytes 772
  108.8 30.2 %collective-permute-start.4 = (f32[182,64]{1,0:T(8,128)}, f32[182,64]{1,0:T(8,128)S(1)}, u32[]{:S(2)}, u32[]{:S(2)}) collective-permute-start(f32[182,64]{1,0:T(8,128)} %get-tuple-element.78), channel_id=1, source_target_pairs={{0,504},{8,0},{16,8},{24,16},{32,24},{40,32},{48,40},{56,48},{64,5... | collective-permute-start | bytes 139784 | tf_op jit(solution)/shard_map/ppermute | solution.py:18
  115.8 23.1 %collective-permute-start.5 = (f32[182,64]{1,0:T(8,128)}, f32[182,64]{1,0:T(8,128)S(1)}, u32[]{:S(2)}, u32[]{:S(2)}) collective-permute-start(f32[182,64]{1,0:T(8,128)} %get-tuple-element.79), channel_id=1, source_target_pairs={{0,8},{8,16},{16,24},{24,32},{32,40},{40,48},{48,56},{56,64},{64,7... | collective-permute-start | bytes 139784 | tf_op jit(solution)/shard_map/ppermute | solution.py:18
  120.7 4.0 %copy-start.3 = (f32[5,6,6,64]{3,1,2,0:T(8,128)}, f32[5,6,6,64]{3,1,2,0:T(8,128)S(1)}, u32[]{:S(2)}) copy-start(f32[5,6,6,64]{3,1,2,0:T(8,128)S(1)} %constant_dynamic-update-slice_fusion.35) | copy-start | bytes 138244
  122.6 2.2 copy-start.2
  124.7 1.4 copy-start.1
  124.8 1.4 copy-start.11
  130.8 1.3 copy-start.6
  132.1 3.3 %copy-start.14 = (f32[256]{0:T(256)S(1)}, f32[256]{0:T(256)}, u32[]{:S(2)}) copy-start(f32[256]{0:T(256)} %get-tuple-element.91) | copy-start | bytes 3076
  148.6 9.2 %collective-permute-start.6 = (f32[180,64]{1,0:T(8,128)S(1)}, f32[180,64]{1,0:T(8,128)S(1)}, u32[]{:S(2)}, u32[]{:S(2)}) collective-permute-start(f32[180,64]{1,0:T(8,128)S(1)} %get-tuple-element.75), channel_id=1, source_target_pairs={{0,8},{8,16},{16,24},{24,32},{32,40},{40,48},{48,56},{56,64},{64,7... | collective-permute-start | bytes 138248 | tf_op jit(solution)/shard_map/ppermute | solution.py:18
  150.5 8.3 %collective-permute-start.7 = (f32[180,64]{1,0:T(8,128)S(1)}, f32[180,64]{1,0:T(8,128)S(1)}, u32[]{:S(2)}, u32[]{:S(2)}) collective-permute-start(f32[180,64]{1,0:T(8,128)S(1)} %get-tuple-element.76), channel_id=1, source_target_pairs={{0,504},{8,0},{16,8},{24,16},{32,24},{40,32},{48,40},{56,48},{64,5... | collective-permute-start | bytes 138248 | tf_op jit(solution)/shard_map/ppermute | solution.py:18
  161.3 2.7 %copy-start.9 = (f32[64]{0:T(128)S(1)}, f32[64]{0:T(128)}, u32[]{:S(2)}) copy-start(f32[64]{0:T(128)} %get-tuple-element.94) | copy-start | bytes 772
  166.6 1.6 copy-start.4
  171.4 7.9 %copy-start.15 = (f32[256]{0:T(256)S(1)}, f32[256]{0:T(256)}, u32[]{:S(2)}) copy-start(f32[256]{0:T(256)} %get-tuple-element.91) | copy-start | bytes 3076
  177.3 2.3 %copy-start.12 = (s32[256]{0:T(256)S(1)}, s32[256]{0:T(256)}, u32[]{:S(2)}) copy-start(s32[256]{0:T(256)} %param.25) | copy-start | bytes 3076
Sparse Core Ops, SparseCore 0:
  180.9 33.4 reduce-scatter.1
where the time goes:
time: 226 us; the launch traced here: 221 us
  local copies, waits for them, and re-layouts  46.6 us (21%)
  other arithmetic  46 us (20%)
  starting transfers between devices  43.4 us (19%)
  matrix products  37.6 us (17%)
  waiting for transfers between devices  31.7 us (14%)
  between operations  16.1 us (7%)
    ppermute x8, starting transfers between devices, shifted(): return lax.ppermute(value, axis, pairs)  43.4 us
    reduce_scatter x1, waiting for transfers between devices, local(): lax.psum_scatter(partial_sums, 'span', scatter_dimension=1, tiled=True)  29.7 us
    unnamed x37, other arithmetic  20.3 us
    scatter-add x2, local copies, waits for them, and re-layouts, residual(): volume = volume.at[:, :, :, 0, face_count:2 * face_count].add(stator_lift)  13.1 us
    dot_general x2, matrix products, volume_term(): jnp.einsum('ai,vijke->vajke', deriv_table, fields, precision=lax.Precisio...  6.33 us
    dot_general x2, matrix products, residual(): jnp.dot(stator_terms, offset_hot.T, precision=lax.Precision.HIGHEST)  6.32 us
    scatter-add x3, local copies, waits for them, and re-layouts, residual(): volume = volume.at[:, :, :, 5, :face_count].add(rotor_lift)  5.08 us
    dot_general x2, matrix products, volume_term(): jnp.einsum('bj,vijke->vibke', deriv_table, fields, precision=lax.Precisio...  4.73 us
  transfers between devices with their start and end apart: 9, of which 3 were waited for; matrix products, arithmetic and copies ran while one was open for 20% of the time, Pallas kernels for 0%

commit v1 on v0

v1 whole, which is shorter than its diff:
```python
import jax
import jax.numpy as jnp
import numpy as np
from jax import lax
from jax.experimental import pallas as pl
from jax.experimental.pallas import tpu as pltpu
from jax.sharding import PartitionSpec as P

NP = 6
NV = 5
FACES = 64
LANES = 128
ROWS = NV * NP * NP
CODES, FIRST, SECOND, ONES = ROWS, ROWS + 1, ROWS + 2, ROWS + 3
MSG = ROWS + 4

time_step = 0.02
lift_scale = 15.0

PARTNERS = ({0: 1, 1: 4, 4: 1}, {0: 2, 2: 4, 4: 2}, {0: 3, 3: 4, 4: 3})


def node_table():
    return np.array(
        [
            -1.0,
            -0.7650553239294647,
            -0.2852315164806451,
            0.2852315164806451,
            0.7650553239294647,
            1.0,
        ]
    )


def weight_table():
    return np.array(
        [
            1.0 / 15.0,
            0.378474956297847,
            0.5548583770354863,
            0.5548583770354863,
            0.378474956297847,
            1.0 / 15.0,
        ]
    )


def derivative_table():
    nodes = node_table()
    count = nodes.shape[0]
    barycentric = np.ones(count)
    for first in range(count):
        for other in range(count):
            if other != first:
                barycentric[first] = barycentric[first] / (nodes[first] - nodes[other])
    table = np.zeros((count, count))
    for row_index in range(count):
        for col_index in range(count):
            if row_index != col_index:
                table[row_index, col_index] = (
                    barycentric[col_index]
                    / barycentric[row_index]
                    / (nodes[row_index] - nodes[col_index])
                )
        table[row_index, row_index] = -np.sum(table[row_index])
    return table


DERIV = derivative_table()
ODD = [[0.5 * float(DERIV[a, m] - DERIV[a, 5 - m]) for m in range(3)] for a in range(3)]
EVEN = [[0.5 * float(DERIV[a, m] + DERIV[a, 5 - m]) for m in range(3)] for a in range(3)]
COARSE = [[float(w) for w in row] for row in (weight_table(), weight_table() * node_table())]


def derivative(tiles):
    even = [tiles[m] + tiles[5 - m] for m in range(3)]
    odd = [tiles[m] - tiles[5 - m] for m in range(3)]
    result = [None] * 6
    for a in range(3):
        s = ODD[a][0] * odd[0] + ODD[a][1] * odd[1] + ODD[a][2] * odd[2]
        d = EVEN[a][0] * even[0] + EVEN[a][1] * even[1] + EVEN[a][2] * even[2]
        result[a] = s + d
        result[5 - a] = s - d
    return result


def moments(tiles):
    even = [tiles[m] + tiles[5 - m] for m in range(3)]
    odd = [tiles[m] - tiles[5 - m] for m in range(3)]
    return [
        COARSE[0][0] * even[0] + COARSE[0][1] * even[1] + COARSE[0][2] * even[2],
        COARSE[1][0] * odd[0] + COARSE[1][1] * odd[1] + COARSE[1][2] * odd[2],
    ]


def flux_tiles(direction, v, speed, load):
    tiles = load(v)
    partner = PARTNERS[direction].get(v)
    if partner is None:
        return [speed * t for t in tiles]
    return [speed * t + o for t, o in zip(tiles, load(partner))]


def column(values):
    at = lax.broadcasted_iota(jnp.int32, (6, 1), 0)
    result = jnp.full((6, 1), values[0], jnp.float32)
    for k in range(1, 6):
        result = jnp.where(at == k, values[k], result)
    return result


def tile(v, i, j):
    return ((v * NP + i) * NP + j) * 8


def volume_passes(flow_ref, q, acc, finish):
    u = [flow_ref[d] for d in range(3)]

    for i in range(NP):
        def load(v, i=i):
            return [q[pl.ds(tile(v, i, 0) + k, 6, stride=8), :] for k in range(6)]

        for v in range(NV):
            out = derivative(flux_tiles(2, v, u[2], load))
            for k in range(6):
                acc[pl.ds(tile(v, i, 0) + k, 6, stride=8), :] = out[k]

    for j in range(NP):
        def load(v, j=j):
            return [q[pl.ds(tile(v, i, j), 8), :] for i in range(6)]

        for v in range(NV):
            out = derivative(flux_tiles(0, v, u[0], load))
            for i in range(6):
                acc[pl.ds(tile(v, i, j), 8), :] += out[i]

    for v in range(NV):
        for i in range(NP):
            def load(w, i=i):
                return [q[pl.ds(tile(w, i, j), 8), :] for j in range(6)]

            out = derivative(flux_tiles(1, v, u[1], load))
            finish(v, i, [acc[pl.ds(tile(v, i, j), 8), :] + out[j] for j in range(6)])


def message_kernel(here_ref, fields_ref, owner_ref, mortar_ref, message_ref):
    lane = lax.broadcasted_iota(jnp.int32, (NP, LANES), 1)
    rotor = lane < FACES
    for v in range(NV):
        for i in range(NP):
            block = fields_ref[v, i]
            message_ref[pl.ds((v * NP + i) * NP, 6), :] = jnp.where(
                rotor, block[:, 5, :], block[:, 0, :]
            )
    sectors = here_ref[1]
    step = owner_ref[...] - here_ref[0]
    after = (step == 1) | (step == 1 - sectors)
    side = jnp.where(step == 0, 1, jnp.where(after, 2, 0))
    code = (side * FACES + mortar_ref[...]).astype(jnp.float32)
    source = lax.broadcasted_iota(jnp.int32, (LANES, 3 * LANES), 0)
    target = lax.broadcasted_iota(jnp.int32, (LANES, 3 * LANES), 1)
    face = target % FACES
    half = jnp.where(target < LANES, (target // FACES) % 2, target // LANES - 1)
    select = (source == 2 * face + half).astype(jnp.float32).astype(jnp.bfloat16)
    code = jnp.broadcast_to(code, (8, LANES)).astype(jnp.bfloat16)
    rows = jnp.dot(code, select, preferred_element_type=jnp.float32)
    message_ref[CODES : CODES + 1, :] = rows[0:1, 0:LANES]
    message_ref[FIRST : FIRST + 1, :] = rows[0:1, LANES : 2 * LANES]
    message_ref[SECOND : SECOND + 1, :] = rows[0:1, 2 * LANES : 3 * LANES]
    message_ref[ONES : ONES + 1, :] = jnp.ones((1, LANES), jnp.float32)


def coefficient_rows(mats_ref, table_ref):
    lane = lax.broadcasted_iota(jnp.int32, (1, LANES), 1)
    rotor = lane < FACES

    def entry(side, h, a, i):
        return mats_ref[((side * 2 + h) * NP + a) * NP + i]

    for h in range(2):
        own = [
            [jnp.where(rotor, entry(0, h, a, i), entry(1, h, a, i)) for i in range(6)]
            for a in range(6)
        ]
        other = [
            [jnp.where(rotor, entry(1, h, a, i), entry(0, h, a, i)) for i in range(6)]
            for a in range(6)
        ]
        for i in range(6):
            for m in range(6):
                cross = own[i][0] * other[0][m]
                square = own[i][0] * own[0][m]
                for a in range(1, 6):
                    cross = cross + own[i][a] * other[a][m]
                    square = square + own[i][a] * own[a][m]
                row = h * 36 + i * 6 + m
                table_ref[row : row + 1, :] = cross
                table_ref[72 + row : 73 + row, :] = square


def first_volume_kernel(
    flow_ref, mats_ref, fields_ref, jac_ref, rate_ref, trace_ref, table_ref, q, acc
):
    for v in range(NV):
        for i in range(NP):
            for j in range(NP):
                q[pl.ds(tile(v, i, j), 6), :] = fields_ref[v, i, j]
    scale = -time_step * jac_ref[...]

    def finish(v, i, tiles):
        for j in range(6):
            value = scale * tiles[j]
            rate_ref[v, i, j] = value[0:6]
            acc[pl.ds(tile(v, i, j), 8), :] = value

    volume_passes(flow_ref, q, acc, finish)

    @pl.when(pl.program_id(0) == 0)
    def _():
        lane = lax.broadcasted_iota(jnp.int32, (NP, LANES), 1)
        rotor = lane < FACES
        for v in range(NV):
            for i in range(NP):
                at = tile(v, i, 0)
                top = pl.ds(at + 5, 6, stride=8)
                bottom = pl.ds(at, 6, stride=8)
                trace_ref[pl.ds((v * NP + i) * NP, 6), :] = jnp.where(
                    rotor, q[top, :] + acc[top, :], q[bottom, :] + acc[bottom, :]
                )
        coefficient_rows(mats_ref, table_ref)


def layer_mask():
    node = lax.broadcasted_iota(jnp.int32, (NP, LANES), 0)
    lane = lax.broadcasted_iota(jnp.int32, (NP, LANES), 1)
    hit = ((node == 5) & (lane < FACES)) | ((node == 0) & (lane >= FACES))
    return jnp.where(hit, 1.0, 0.0)


def second_volume_kernel(
    flow_ref, fields_ref, jac_ref, rate_ref, lift_ref, new_ref, modes_ref, q, acc
):
    mask = layer_mask() * jnp.where(pl.program_id(0) == 0, 1.0, 0.0)
    for v in range(NV):
        for i in range(NP):
            for j in range(NP):
                row = (v * NP + i) * NP + j
                layer = jnp.broadcast_to(lift_ref[row : row + 1, :], (NP, LANES))
                q[pl.ds(tile(v, i, j), 6), :] = (
                    fields_ref[v, i, j] + rate_ref[v, i, j] + mask * layer
                )
    jac = jac_ref[...]
    scale = -time_step * jac
    weight = (0.5 / time_step) / (jac * jac * jac)
    columns = [column(COARSE[c]) for c in range(2)]
    sums = {}

    def finish(v, i, tiles):
        change = []
        for j in range(6):
            base = fields_ref[v, i, j]
            first = q[pl.ds(tile(v, i, j), 6), :] - base
            both = first + scale * tiles[j][0:6]
            new_ref[v, i, j] = base + 0.5 * both
            change.append(both)
        for b, value in enumerate(moments(change)):
            for a in range(2):
                term = COARSE[a][i] * value
                sums[a, b] = term if i == 0 else sums[a, b] + term
        if i == 5:
            for a in range(2):
                for b in range(2):
                    for c in range(2):
                        row = v * 8 + a * 4 + b * 2 + c
                        total = jnp.sum(columns[c] * sums[a, b], axis=0, keepdims=True)
                        modes_ref[row : row + 1, :] = weight * total

    volume_passes(flow_ref, q, acc, finish)


def split(value):
    high = value.astype(jnp.bfloat16)
    low = (value - high.astype(jnp.float32)).astype(jnp.bfloat16)
    return high, low


def pair_matrix(left_ref, own_ref, right_ref, pick):
    lane = lax.broadcasted_iota(jnp.int32, (FACES, LANES), 1)
    face = lax.broadcasted_iota(jnp.int32, (FACES, LANES), 0).astype(jnp.float32)
    stator = lane >= FACES
    own = [own_ref[row : row + 1, :] for row in (FIRST, SECOND)]
    for device, ref in enumerate((left_ref, own_ref, right_ref)):
        code = jnp.broadcast_to(ref[CODES : CODES + 1, :], (LANES, LANES)).T
        offset = (2 - device) * FACES
        target = jnp.where(stator, lane - FACES + offset, -1).astype(jnp.float32)
        for h in range(2):
            top = jnp.where(code[h * FACES : (h + 1) * FACES] == target, 1.0, 0.0)
            mine = jnp.where(stator, -1.0, jnp.broadcast_to(own[h], (FACES, LANES)))
            bottom = jnp.where(mine == face + float(device * FACES), 1.0, 0.0)
            columns = slice(h * LANES, (h + 1) * LANES)
            at = device * LANES
            pick[at : at + FACES, columns] = top.astype(jnp.bfloat16)
            pick[at + FACES : at + LANES, columns] = bottom.astype(jnp.bfloat16)


def lift_rows(flow_ref, left_ref, own_ref, right_ref, pick, table_ref, jac_ref, work, coef, emit):
    high, low = split(
        jnp.concatenate([left_ref[...], own_ref[...], right_ref[...]], axis=1)
    )
    matrix = pick[...]
    work[...] = jnp.dot(high, matrix, preferred_element_type=jnp.float32) + jnp.dot(
        low, matrix, preferred_element_type=jnp.float32
    )
    coef[...] = (
        work[ONES : ONES + 1, 0:LANES] * table_ref[72:108, :]
        + work[ONES : ONES + 1, LANES : 2 * LANES] * table_ref[108:144, :]
    )
    axial = flow_ref[2]
    speed = 0.5 * (jnp.abs(axial) + 1.0)
    lane = lax.broadcasted_iota(jnp.int32, (1, LANES), 1)
    scale = (time_step * lift_scale) * jac_ref[:, 0:LANES]
    signed = jnp.where(lane < FACES, scale, -scale)
    damp = speed * scale
    for i in range(NP):
        cross = [
            [table_ref[h * 36 + i * 6 + m : h * 36 + i * 6 + m + 1, :] for m in range(6)]
            for h in range(2)
        ]
        square = [coef[i * 6 + m : i * 6 + m + 1, :] for m in range(6)]
        mean, jump = [], []
        for v in range(NV):
            other = None
            own = None
            for m in range(6):
                rows = pl.ds((v * NP + m) * NP, 6)
                term = cross[0][m] * work[rows, 0:LANES]
                term = term + cross[1][m] * work[rows, LANES : 2 * LANES]
                other = term if other is None else other + term
                term = square[m] * own_ref[rows, :]
                own = term if own is None else own + term
            mean.append(own_ref[pl.ds((v * NP + i) * NP, 6), :] - 0.5 * (own + other))
            jump.append(own - other)
        for v in range(NV):
            flux = axial * mean[v]
            partner = PARTNERS[2].get(v)
            if partner is not None:
                flux = flux + mean[partner]
            emit(v, i, signed * flux - damp * jump[v])


def first_lift_kernel(
    flow_ref, left_ref, own_ref, right_ref, trace_ref, table_ref, jac_ref,
    message_ref, lift_ref, pick, work, coef,
):
    pair_matrix(left_ref, own_ref, right_ref, pick)

    def emit(v, i, value):
        rows = pl.ds((v * NP + i) * NP, 6)
        lift_ref[rows, :] = value
        message_ref[rows, :] = trace_ref[rows, :] + value

    lift_rows(
        flow_ref, left_ref, own_ref, right_ref, pick, table_ref, jac_ref, work, coef, emit
    )
    message_ref[ROWS:MSG, :] = own_ref[ROWS:MSG, :]


def second_lift_kernel(
    flow_ref, left_ref, own_ref, right_ref, pick, table_ref, jac_ref, modes_ref, agg_ref, base_ref,
    new_ref, sums_ref, work, coef,
):
    mask = 0.5 * layer_mask()
    sums = {}

    def emit(v, i, value):
        for j in range(6):
            new_ref[v, i, j] = base_ref[v, i, j] + mask * jnp.broadcast_to(
                value[j : j + 1, :], (NP, LANES)
            )
        for a in range(2):
            term = COARSE[a][i] * value
            sums[v, a] = term if i == 0 else sums[v, a] + term

    lift_rows(
        flow_ref, left_ref, own_ref, right_ref, pick, table_ref, jac_ref, work, coef, emit
    )
    lane = lax.broadcasted_iota(jnp.int32, (1, LANES), 1)
    jac = jac_ref[:, 0:LANES]
    weight = (0.5 / time_step) / (jac * jac * jac)
    ends = [weight * jnp.where(lane < FACES, COARSE[c][5], COARSE[c][0]) for c in range(2)]
    columns = [column(COARSE[b]) for b in range(2)]
    rows = []
    for v in range(NV):
        for a in range(2):
            for b in range(2):
                total = jnp.sum(columns[b] * sums[v, a], axis=0, keepdims=True)
                for c in range(2):
                    rows.append(ends[c] * total)
    count = 8 * NV
    at = lax.broadcasted_iota(jnp.int32, (8, LANES), 0)
    blocks = []
    for v in range(NV):
        block = jnp.broadcast_to(rows[v * 8], (8, LANES))
        for r in range(1, 8):
            block = jnp.where(at == r, rows[v * 8 + r], block)
        blocks.append(block)
    faces = modes_ref[:, 0:LANES] + jnp.concatenate(blocks, axis=0)
    modes = jnp.concatenate([faces, modes_ref[:, LANES:]], axis=1)
    high, low = split(modes)
    aggs = sums_ref.shape[0] * sums_ref.shape[1]
    name = lax.broadcasted_iota(jnp.int32, (aggs, modes.shape[1]), 0)
    member = jnp.where(name == agg_ref[...], 1.0, 0.0).astype(jnp.bfloat16)
    contract = (((1,), (1,)), ((), ()))
    total = lax.dot_general(
        member, high, contract, preferred_element_type=jnp.float32
    ) + lax.dot_general(member, low, contract, preferred_element_type=jnp.float32)
    share = sums_ref.shape[1]
    for s in range(sums_ref.shape[0]):
        sums_ref[s] = total[s * share : (s + 1) * share, :]


def shifted(value, axis, steps):
    count = lax.axis_size(axis)
    pairs = [(source, (source + steps) % count) for source in range(count)]
    return lax.ppermute(value, axis, pairs)


VMEM = pl.BlockSpec(memory_space=pltpu.VMEM)
SMEM = pl.BlockSpec(memory_space=pltpu.SMEM)


def shape(*dims, dtype=jnp.float32):
    return jax.ShapeDtypeStruct(dims, dtype)


def params():
    return pltpu.CompilerParams(vmem_limit_bytes=48 * 1024 * 1024)


def local(fields, jacobian, mean_flow, pair_owner, pair_mortar, mortar_proj, coarse_id):
    elements = fields.shape[4]
    spans = lax.axis_size("span")
    aggs = elements * spans // 8
    jac_row = jacobian.reshape(1, elements)
    mats = mortar_proj.reshape(4 * NP * NP)
    here = jnp.stack([lax.axis_index("blk"), lax.axis_size("blk")]).astype(jnp.int32)
    dims = (NV, NP, NP, NP, LANES)
    half = pl.BlockSpec(dims, lambda n: (0, 0, 0, 0, n))
    row = pl.BlockSpec((1, LANES), lambda n: (0, n))
    whole = pl.BlockSpec((MSG, LANES), lambda n: (0, 0))
    face_half = pl.BlockSpec(dims, lambda n: (0, 0, 0, 0, 0))
    fixed = lambda *d: pl.BlockSpec(d, lambda n: (0,) * len(d))
    tiles = pltpu.VMEM((NV * NP * NP * 8, LANES), jnp.float32)
    grid = (elements // LANES,)
    volume_cost = pl.CostEstimate(
        flops=120 * NV * 216 * elements, bytes_accessed=3 * 4 * 1440 * elements, transcendentals=0
    )

    message = pl.pallas_call(
        message_kernel,
        grid=(1,),
        in_specs=[SMEM, face_half, fixed(1, LANES), fixed(1, LANES)],
        out_specs=whole,
        out_shape=shape(MSG, LANES),
        compiler_params=params(),
        name="face_message",
    )(here, fields, pair_owner.reshape(1, LANES), pair_mortar.reshape(1, LANES))
    left = shifted(message, "blk", 1)
    right = shifted(message, "blk", -1)

    rate, trace, table = pl.pallas_call(
        first_volume_kernel,
        grid=grid,
        in_specs=[SMEM, SMEM, half, row],
        out_specs=[half, whole, fixed(144, LANES)],
        out_shape=[shape(*fields.shape), shape(MSG, LANES), shape(144, LANES)],
        scratch_shapes=[tiles, tiles],
        compiler_params=params(),
        cost_estimate=volume_cost,
        name="first_volume",
    )(mean_flow, mats, fields, jac_row)

    message2, lift, pick = pl.pallas_call(
        first_lift_kernel,
        in_specs=[SMEM] + [VMEM] * 6,
        out_specs=[VMEM] * 3,
        out_shape=[
            shape(MSG, LANES),
            shape(ROWS, LANES),
            shape(3 * LANES, 2 * LANES, dtype=jnp.bfloat16),
        ],
        scratch_shapes=[
            pltpu.VMEM((MSG, 2 * LANES), jnp.float32),
            pltpu.VMEM((36, LANES), jnp.float32),
        ],
        compiler_params=params(),
        name="first_lift",
    )(mean_flow, left, message, right, trace, table, jac_row)
    left2 = shifted(message2, "blk", 1)
    right2 = shifted(message2, "blk", -1)

    base, modes = pl.pallas_call(
        second_volume_kernel,
        grid=grid,
        in_specs=[SMEM, half, row, half, fixed(ROWS, LANES)],
        out_specs=[half, pl.BlockSpec((8 * NV, LANES), lambda n: (0, n))],
        out_shape=[shape(*fields.shape), shape(8 * NV, elements)],
        scratch_shapes=[tiles, tiles],
        compiler_params=params(),
        cost_estimate=volume_cost,
        name="second_volume",
    )(mean_flow, fields, jac_row, rate, lift)

    new_fields, sums = pl.pallas_call(
        second_lift_kernel,
        grid=(1,),
        in_specs=[
            SMEM,
            whole,
            whole,
            whole,
            fixed(3 * LANES, 2 * LANES),
            fixed(144, LANES),
            fixed(1, elements),
            fixed(8 * NV, elements),
            fixed(1, elements),
            face_half,
        ],
        out_specs=[face_half, fixed(spans, aggs // spans, 8 * NV)],
        out_shape=[shape(*fields.shape), shape(spans, aggs // spans, 8 * NV)],
        scratch_shapes=[
            pltpu.VMEM((MSG, 2 * LANES), jnp.float32),
            pltpu.VMEM((36, LANES), jnp.float32),
        ],
        input_output_aliases={9: 0},
        compiler_params=params(),
        name="second_lift",
    )(
        mean_flow, left2, message2, right2, pick, table, jac_row, modes,
        coarse_id.reshape(1, elements), base,
    )
    parts = lax.all_to_all(sums, "span", 0, 0)
    return new_fields, jnp.sum(parts, axis=0).T


def solution(mesh):
    return jax.shard_map(
        local,
        mesh=mesh,
        in_specs=(
            P(None, None, None, None, ("blk", "span")),
            P(("blk", "span")),
            P(),
            P(("blk", "span"), None),
            P(("blk", "span")),
            P(),
            P(("blk", "span")),
        ),
        out_specs=(P(None, None, None, None, ("blk", "span")), P(None, ("blk", "span"))),
        check_vma=False,
    )
```

time: 226 us -> 52.7 us (0.23); the launches traced: 221 us -> 52.4 us
  other arithmetic: 46 us -> 1.44 us
  local copies, waits for them, and re-layouts: 46.6 us -> 3.57 us
  matrix products: 37.6 us -> 0 us
  waiting for transfers between devices: 31.7 us -> 0.01 us
  starting transfers between devices: 43.4 us -> 24.7 us
  between operations: 16.1 us -> 0.8 us
  Pallas kernels: 0 us -> 11.4 us
  blocking collectives: 0 us -> 10.5 us
    dot_general x38 -> x0, matrix products: 37.6 us -> none  [the longest x2 6.33 us: volume_term(): jnp.einsum('ai,vijke->vajke', deriv_table, fields, precision=lax.Precisio...]
    reduce_scatter x1 -> x0, waiting for transfers between devices: 29.7 us -> none  [local(): lax.psum_scatter(partial_sums, 'span', scatter_dimension=1, tiled=True)]
    unnamed x37 -> x0, other arithmetic: 20.3 us -> none
    ppermute x8 -> x4, starting transfers between devices: 43.4 us -> 24.7 us  [shifted(): return lax.ppermute(value, axis, pairs)]
    scatter-add x5 -> x0, local copies, waits for them, and re-layouts: 18.1 us -> none  [the longest x2 13.1 us: residual(): volume = volume.at[:, :, :, 0, face_count:2 * face_count].add(stator_lift)]
    pallas_call x0 -> x5, Pallas kernels: none -> 11.4 us  [the longest x1 3.87 us: local(): pl.pallas_call(second_volume_kernel, grid=grid, in_specs=[SMEM, half, row...]
    all_to_all x0 -> x1, blocking collectives: none -> 10.5 us  [local(): parts = lax.all_to_all(sums, 'span', 0, 0)]
    add x5 -> x0, other arithmetic: 6.74 us -> none  [the longest x1 2.43 us: local(): new_fields = 0.5 * fields + 0.5 * (section_one + time_step * second_rate)]
  transfers between devices with their start and end apart: 9 -> 4, of which waited for: 3 -> 0; matrix products, arithmetic and copies ran while one was open for 20% -> 0% of each run, Pallas kernels for 0% -> 13%
where the time goes in v1:
time: 52.7 us; the launch traced here: 52.4 us
  starting transfers between devices  24.7 us (47%)
  Pallas kernels  11.4 us (22%)
  blocking collectives  10.5 us (20%)
  local copies, waits for them, and re-layouts  3.57 us (7%)
  other arithmetic  1.44 us (3%)
  between operations  0.8 us (2%)
    ppermute x4, starting transfers between devices, shifted(): return lax.ppermute(value, axis, pairs)  24.7 us
    all_to_all x1, blocking collectives, local(): parts = lax.all_to_all(sums, 'span', 0, 0)  10.5 us
    pallas_call x1, Pallas kernels, local(): pl.pallas_call(second_volume_kernel, grid=grid, in_specs=[SMEM, half, row...  3.87 us
    unnamed x19, local copies, waits for them, and re-layouts  2.97 us
    pallas_call x1, Pallas kernels, local(): pl.pallas_call(first_volume_kernel, grid=grid, in_specs=[SMEM, SMEM, half...  2.83 us
    pallas_call x1, Pallas kernels, local(): pl.pallas_call(second_lift_kernel, grid=(1,), in_specs=[SMEM, whole, whol...  2.72 us
    pallas_call x1, Pallas kernels, local(): pl.pallas_call(first_lift_kernel, in_specs=[SMEM] + [VMEM] * 6, out_specs...  1.2 us
  transfers between devices with their start and end apart: 4, of which 0 were waited for; matrix products, arithmetic and copies ran while one was open for 0% of the time, Pallas kernels for 13%

profile of v1, /device:TPU:1, one launch (start us, length us, event | category | flops | bytes accessed | tf_op | source)
XLA Modules:
  0.0 52.4 jit_solution(6403736824915162982)
XLA Ops:
  0.6 0.0 copy-start.7
  0.6 0.0 copy-start.2
  0.7 0.0 copy-start.3
  0.7 0.1 pad_add_fusion.here_ref
  0.7 0.0 copy-start
  0.7 1.4 %copy-done = f32[5,6,6,6,256]{4,3,2,1,0:T(8,128)S(1)} copy-done((f32[5,6,6,6,256]{4,3,2,1,0:T(8,128)S(1)}, f32[5,6,6,6,256]{4,3,2,1,0:T(8,128)}, u32[]{:S(2)}) %copy-start) | copy-done | bytes 1105944
  2.1 0.0 copy-start.5
  2.1 0.7 %copy-done.5 = s32[128,1]{0,1:T(1,128)S(1)} copy-done((s32[128,1]{0,1:T(1,128)S(1)}, s32[128,1]{0,1:T(1,128)}, u32[]{:S(2)}) %copy-start.5) | copy-done | bytes 536
  2.8 0.0 copy-start.6
  2.8 0.7 %copy-done.6 = s32[128]{0:T(128)S(1)} copy-done((s32[128]{0:T(128)S(1)}, s32[128]{0:T(128)}, u32[]{:S(2)}) %copy-start.6) | copy-done | bytes 536
  3.4 0.0 copy-start.1
  3.4 0.8 %face_message.1.own_ref = f32[184,128]{1,0:T(8,128)S(1)} custom-call(s32[2]{0:T(128)S(1)} %pad_add_fusion.here_ref, f32[5,6,6,6,256]{4,3,2,1,0:T(8,128)S(1)} %copy-done, s32[1,128]{1,0:T(1,128)S(1)} %bitcast.11, s32[1,128]{1,0:T(1,128)S(1)} %bitcast.12), custom_call_target="tpu_custom_call" | custom-call | tf_op jit(solution)/shard_map/face_message/pallas_call | solution.py:460
  4.2 4.4 %collective-permute-start = (f32[184,128]{1,0:T(8,128)S(1)}, f32[184,128]{1,0:T(8,128)S(1)}, u32[]{:S(2)}, u32[]{:S(2)}) collective-permute-start(f32[184,128]{1,0:T(8,128)S(1)} %face_message.1.own_ref), channel_id=1, source_target_pairs={{0,8},{8,16},{16,24},{24,32},{32,40},{40,48},{48,56},{56,64},{64,7... | collective-permute-start | bytes 282632 | tf_op jit(solution)/shard_map/ppermute | solution.py:426
  8.6 11.7 %collective-permute-start.1 = (f32[184,128]{1,0:T(8,128)S(1)}, f32[184,128]{1,0:T(8,128)S(1)}, u32[]{:S(2)}, u32[]{:S(2)}) collective-permute-start(f32[184,128]{1,0:T(8,128)S(1)} %face_message.1.own_ref), channel_id=1, source_target_pairs={{0,504},{8,0},{16,8},{24,16},{32,24},{40,32},{48,40},{56,48},{64,5... | collective-permute-start | bytes 282632 | tf_op jit(solution)/shard_map/ppermute | solution.py:426
  20.3 0.0 copy-done.7
  20.3 0.1 reshape.21.mats_ref
  20.4 0.0 copy-done.2
  20.4 0.0 copy-done.3
  20.4 0.0 copy-done.1
  20.4 2.8 %first_volume.1 = (f32[5,6,6,6,256]{4,3,2,1,0:T(8,128)S(1)}, f32[184,128]{1,0:T(8,128)S(1)}, f32[144,128]{1,0:T(8,128)S(1)}) custom-call(f32[3]{0:T(128)S(1)} %copy-done.3, f32[144]{0:T(256)S(1)} %reshape.21.mats_ref, f32[5,6,6,6,256]{4,3,2,1,0:T(8,128)S(1)} %copy-done.1, f32[1,256]{1,0:T(1,128)S(1)} %bitcast.6), custom_call_target="tpu_custom_call" | custom-call | flops 33177600 | bytes 4423680 | tf_op jit(solution)/shard_map/first_volume/pallas_call | solution.py:472
  23.3 0.0 collective-permute-done.left_ref
  23.3 0.0 collective-permute-done.1.right_ref
  23.3 1.2 %first_lift.1 = (f32[184,128]{1,0:T(8,128)S(1)}, f32[180,128]{1,0:T(8,128)S(1)}, bf16[384,256]{1,0:T(8,128)(2,1)S(1)}) custom-call(f32[3]{0:T(128)S(1)} %copy-done.3, f32[184,128]{1,0:T(8,128)S(1)} %collective-permute-done.left_ref, f32[184,128]{1,0:T(8,128)S(1)} %face_message.1.own_ref, f32[184,128]{1,0:T(8,128)S(1)} %collective-permute-done.1.right_ref, ...), custom_call_target="tpu_custom_call" | custom-call | tf_op jit(solution)/shard_map/first_lift/pallas_call | solution.py:484
  24.5 1.9 %collective-permute-start.2 = (f32[184,128]{1,0:T(8,128)S(1)}, f32[184,128]{1,0:T(8,128)S(1)}, u32[]{:S(2)}, u32[]{:S(2)}) collective-permute-start(f32[184,128]{1,0:T(8,128)S(1)} %get-tuple-element.14.own_ref), channel_id=1, source_target_pairs={{0,8},{8,16},{16,24},{24,32},{32,40},{40,48},{48,56},{56,64},{64,7... | collective-permute-start | bytes 282632 | tf_op jit(solution)/shard_map/ppermute | solution.py:426
  26.4 6.7 %collective-permute-start.3 = (f32[184,128]{1,0:T(8,128)S(1)}, f32[184,128]{1,0:T(8,128)S(1)}, u32[]{:S(2)}, u32[]{:S(2)}) collective-permute-start(f32[184,128]{1,0:T(8,128)S(1)} %get-tuple-element.14.own_ref), channel_id=1, source_target_pairs={{0,504},{8,0},{16,8},{24,16},{32,24},{40,32},{48,40},{56,48},{64,5... | collective-permute-start | bytes 282632 | tf_op jit(solution)/shard_map/ppermute | solution.py:426
  33.1 0.0 copy-start.4
  33.1 3.9 %second_volume.1 = (f32[5,6,6,6,256]{4,3,2,1,0:T(8,128)}, f32[40,256]{1,0:T(8,128)S(1)}) custom-call(f32[3]{0:T(128)S(1)} %copy-done.3, f32[5,6,6,6,256]{4,3,2,1,0:T(8,128)S(1)} %copy-done.1, f32[1,256]{1,0:T(1,128)S(1)} %bitcast.8, f32[5,6,6,6,256]{4,3,2,1,0:T(8,128)S(1)} %get-tuple-element.16.rate_ref, f32[180,128]{1,0:T(8,128)S(1)} %get-tuple-element.17.lift_ref), custom_call_target="tpu_custom_call" | custom-call | flops 33177600 | bytes 4423680 | tf_op jit(solution)/shard_map/second_volume/pallas_call | solution.py:503
  37.0 0.0 collective-permute-done.2.left_ref
  37.0 0.0 collective-permute-done.3.right_ref
  37.0 0.0 copy-done.4
  37.0 2.7 %second_lift.1 = (f32[5,6,6,6,256]{4,3,2,1,0:T(8,128)}, f32[8,32,40]{2,1,0:T(8,128)S(1)}) custom-call(f32[3]{0:T(128)S(1)} %copy-done.3, f32[184,128]{1,0:T(8,128)S(1)} %collective-permute-done.2.left_ref, f32[184,128]{1,0:T(8,128)S(1)} %get-tuple-element.14.own_ref, ...), custom_call_target="tpu_custom_call", output_to_operand_aliasing={{0}: (9, {})} | custom-call | tf_op jit(solution)/shard_map/second_lift/pallas_call | solution.py:515
  39.7 0.1 reshape.24
  39.9 10.5 %all_to_all.5 = f32[8,1,1280]{2,1,0:T(1,128)S(1)} all-to-all(f32[8,1,1280]{2,1,0:T(1,128)S(1)} %reshape.24), channel_id=1, replica_groups=mesh['blk'=64,'span'=8] {'span'}, dimensions={0} | all-to-all | bytes 81920 | tf_op jit(solution)/shard_map/all_to_all | solution.py:543
  50.4 0.5 broadcast
  50.9 0.7 %reduce = f32[8,1280]{1,0:T(8,128)S(1)} reduce(f32[8,1,1280]{2,1,0:T(1,128)S(1)} %all_to_all.5, f32[]{:T(128)} %broadcast), dimensions={1}, to_apply=%all_to_all.3.reduce_sub_computation | reduce | bytes 81924 | tf_op jit(solution)/shard_map/all_to_all | solution.py:543
  51.7 0.1 reshape.25
  51.8 0.6 %reduce_sum.9 = f32[32,40]{1,0:T(8,128)} reduce(f32[8,32,40]{2,1,0:T(8,128)S(1)} %reshape.25, f32[]{:T(128)} %constant.9.clone.1), dimensions={0}, to_apply=%region_0.0 | reduce | flops 8960 | bytes 46084 | tf_op jit(solution)/shard_map/reduce_sum | solution.py:544
  (1 shorter events, 0.0 us)
Async XLA Ops:
  0.6 19.6 %copy-start.7 = (f32[2,2,6,6]{3,1,2,0:T(2,128)S(1)}, f32[2,2,6,6]{3,1,2,0:T(2,128)}, u32[]{:S(2)}) copy-start(f32[2,2,6,6]{3,1,2,0:T(2,128)} %param.12) | copy-start | bytes 1732
  0.6 19.7 %copy-start.2 = (f32[256]{0:T(256)S(1)}, f32[256]{0:T(256)}, u32[]{:S(2)}) copy-start(f32[256]{0:T(256)} %param.8) | copy-start | bytes 3076
  0.7 19.7 %copy-start.3 = (f32[3]{0:T(128)S(1)}, f32[3]{0:T(128)}, u32[]{:S(2)}) copy-start(f32[3]{0:T(128)} %flow_ref.7) | copy-start | bytes 40
  0.7 1.4 %copy-start = (f32[5,6,6,6,256]{4,3,2,1,0:T(8,128)S(1)}, f32[5,6,6,6,256]{4,3,2,1,0:T(8,128)}, u32[]{:S(2)}) copy-start(f32[5,6,6,6,256]{4,3,2,1,0:T(8,128)} %fields_ref.5) | copy-start | bytes 3317764
  2.1 0.7 %copy-start.5 = (s32[128,1]{0,1:T(1,128)S(1)}, s32[128,1]{0,1:T(1,128)}, u32[]{:S(2)}) copy-start(s32[128,1]{0,1:T(1,128)} %param.10) | copy-start | bytes 1540
  2.8 0.7 %copy-start.6 = (s32[128]{0:T(128)S(1)}, s32[128]{0:T(128)}, u32[]{:S(2)}) copy-start(s32[128]{0:T(128)} %param.11) | copy-start | bytes 1540
  3.4 17.0 %copy-start.1 = (f32[5,6,6,6,256]{4,3,2,1,0:T(8,128)S(1)}, f32[5,6,6,6,256]{4,3,2,1,0:T(8,128)}, u32[]{:S(2)}) copy-start(f32[5,6,6,6,256]{4,3,2,1,0:T(8,128)} %fields_ref.5) | copy-start | bytes 3317764
  4.2 19.1 %collective-permute-start = (f32[184,128]{1,0:T(8,128)S(1)}, f32[184,128]{1,0:T(8,128)S(1)}, u32[]{:S(2)}, u32[]{:S(2)}) collective-permute-start(f32[184,128]{1,0:T(8,128)S(1)} %face_message.1.own_ref), channel_id=1, source_target_pairs={{0,8},{8,16},{16,24},{24,32},{32,40},{40,48},{48,56},{56,64},{64,7... | collective-permute-start | bytes 282632 | tf_op jit(solution)/shard_map/ppermute | solution.py:426
  8.6 14.7 %collective-permute-start.1 = (f32[184,128]{1,0:T(8,128)S(1)}, f32[184,128]{1,0:T(8,128)S(1)}, u32[]{:S(2)}, u32[]{:S(2)}) collective-permute-start(f32[184,128]{1,0:T(8,128)S(1)} %face_message.1.own_ref), channel_id=1, source_target_pairs={{0,504},{8,0},{16,8},{24,16},{32,24},{40,32},{48,40},{56,48},{64,5... | collective-permute-start | bytes 282632 | tf_op jit(solution)/shard_map/ppermute | solution.py:426
  24.5 12.5 %collective-permute-start.2 = (f32[184,128]{1,0:T(8,128)S(1)}, f32[184,128]{1,0:T(8,128)S(1)}, u32[]{:S(2)}, u32[]{:S(2)}) collective-permute-start(f32[184,128]{1,0:T(8,128)S(1)} %get-tuple-element.14.own_ref), channel_id=1, source_target_pairs={{0,8},{8,16},{16,24},{24,32},{32,40},{40,48},{48,56},{56,64},{64,7... | collective-permute-start | bytes 282632 | tf_op jit(solution)/shard_map/ppermute | solution.py:426
  26.4 10.6 %collective-permute-start.3 = (f32[184,128]{1,0:T(8,128)S(1)}, f32[184,128]{1,0:T(8,128)S(1)}, u32[]{:S(2)}, u32[]{:S(2)}) collective-permute-start(f32[184,128]{1,0:T(8,128)S(1)} %get-tuple-element.14.own_ref), channel_id=1, source_target_pairs={{0,504},{8,0},{16,8},{24,16},{32,24},{40,32},{48,40},{56,48},{64,5... | collective-permute-start | bytes 282632 | tf_op jit(solution)/shard_map/ppermute | solution.py:426
  33.1 3.9 %copy-start.4 = (s32[256]{0:T(256)S(1)}, s32[256]{0:T(256)}, u32[]{:S(2)}) copy-start(s32[256]{0:T(256)} %param.13) | copy-start | bytes 3076

commit v2 on v1

--- a/solution.py
+++ b/solution.py
@@ -144,7 +144,20 @@
             finish(v, i, [acc[pl.ds(tile(v, i, j), 8), :] + out[j] for j in range(6)])
 
 
-def message_kernel(here_ref, fields_ref, owner_ref, mortar_ref, message_ref):
+def message_kernel(
+    fields_hbm, owner_hbm, mortar_hbm, message_ref, fields_ref, owner_ref, mortar_ref, sems
+):
+    copies = [
+        pltpu.make_async_copy(owner_hbm, owner_ref, sems.at[0]),
+        pltpu.make_async_copy(mortar_hbm, mortar_ref, sems.at[1]),
+        pltpu.make_async_copy(fields_hbm.at[:, :, :, :, pl.ds(0, LANES)], fields_ref, sems.at[2]),
+    ]
+    for copy in copies:
+        copy.start()
+    copies[0].wait()
+    copies[1].wait()
+    pair_codes(owner_ref, mortar_ref, message_ref)
+    copies[2].wait()
     lane = lax.broadcasted_iota(jnp.int32, (NP, LANES), 1)
     rotor = lane < FACES
     for v in range(NV):
@@ -153,8 +166,11 @@
             message_ref[pl.ds((v * NP + i) * NP, 6), :] = jnp.where(
                 rotor, block[:, 5, :], block[:, 0, :]
             )
-    sectors = here_ref[1]
-    step = owner_ref[...] - here_ref[0]
+
+
+def pair_codes(owner_ref, mortar_ref, message_ref):
+    sectors = lax.axis_size("blk")
+    step = owner_ref[...] - lax.axis_index("blk")
     after = (step == 1) | (step == 1 - sectors)
     side = jnp.where(step == 0, 1, jnp.where(after, 2, 0))
     code = (side * FACES + mortar_ref[...]).astype(jnp.float32)
@@ -285,28 +301,33 @@
     return high, low
 
 
-def pair_matrix(left_ref, own_ref, right_ref, pick):
+def pair_matrix(first_ref, own_ref, second_ref, pick):
     lane = lax.broadcasted_iota(jnp.int32, (FACES, LANES), 1)
     face = lax.broadcasted_iota(jnp.int32, (FACES, LANES), 0).astype(jnp.float32)
     stator = lane >= FACES
     own = [own_ref[row : row + 1, :] for row in (FIRST, SECOND)]
-    for device, ref in enumerate((left_ref, own_ref, right_ref)):
+    here = lax.axis_index("blk")
+    side = 2 - 2 * lax.rem(here, 2)
+    for device, (ref, at_side) in enumerate(
+        ((first_ref, side), (own_ref, 1), (second_ref, 2 - side))
+    ):
         code = jnp.broadcast_to(ref[CODES : CODES + 1, :], (LANES, LANES)).T
-        offset = (2 - device) * FACES
+        offset = (2 - at_side) * FACES
+        base = jnp.asarray(at_side * FACES, jnp.int32).astype(jnp.float32)
         target = jnp.where(stator, lane - FACES + offset, -1).astype(jnp.float32)
         for h in range(2):
             top = jnp.where(code[h * FACES : (h + 1) * FACES] == target, 1.0, 0.0)
             mine = jnp.where(stator, -1.0, jnp.broadcast_to(own[h], (FACES, LANES)))
-            bottom = jnp.where(mine == face + float(device * FACES), 1.0, 0.0)
+            bottom = jnp.where(mine == face + base, 1.0, 0.0)
             columns = slice(h * LANES, (h + 1) * LANES)
             at = device * LANES
             pick[at : at + FACES, columns] = top.astype(jnp.bfloat16)
             pick[at + FACES : at + LANES, columns] = bottom.astype(jnp.bfloat16)
 
 
-def lift_rows(flow_ref, left_ref, own_ref, right_ref, pick, table_ref, jac_ref, work, coef, emit):
+def lift_rows(flow_ref, first_ref, own_ref, second_ref, pick, table_ref, jac_ref, work, coef, emit):
     high, low = split(
-        jnp.concatenate([left_ref[...], own_ref[...], right_ref[...]], axis=1)
+        jnp.concatenate([first_ref[...], own_ref[...], second_ref[...]], axis=1)
     )
     matrix = pick[...]
     work[...] = jnp.dot(high, matrix, preferred_element_type=jnp.float32) + jnp.dot(
@@ -350,10 +371,10 @@
 
 
 def first_lift_kernel(
-    flow_ref, left_ref, own_ref, right_ref, trace_ref, table_ref, jac_ref,
+    flow_ref, first_ref, own_ref, second_ref, trace_ref, table_ref, jac_ref,
     message_ref, lift_ref, pick, work, coef,
 ):
-    pair_matrix(left_ref, own_ref, right_ref, pick)
+    pair_matrix(first_ref, own_ref, second_ref, pick)
 
     def emit(v, i, value):
         rows = pl.ds((v * NP + i) * NP, 6)
@@ -361,56 +382,62 @@
         message_ref[rows, :] = trace_ref[rows, :] + value
 
     lift_rows(
-        flow_ref, left_ref, own_ref, right_ref, pick, table_ref, jac_ref, work, coef, emit
+        flow_ref, first_ref, own_ref, second_ref, pick, table_ref, jac_ref, work, coef, emit
     )
     message_ref[ROWS:MSG, :] = own_ref[ROWS:MSG, :]
 
 
 def second_lift_kernel(
-    flow_ref, left_ref, own_ref, right_ref, pick, table_ref, jac_ref, modes_ref, agg_ref, base_ref,
-    new_ref, sums_ref, work, coef,
+    flow_ref, first_ref, own_ref, second_ref, pick, table_ref, jac_ref, modes_ref, agg_ref,
+    base_hbm, new_hbm, sums_ref, work, coef, lift, block, sems,
 ):
-    mask = 0.5 * layer_mask()
+    faces_in = (slice(None),) * 4 + (pl.ds(0, LANES),)
+    fetch = pltpu.make_async_copy(base_hbm.at[faces_in], block, sems.at[0])
+    fetch.start()
+    aggs = sums_ref.shape[0] * sums_ref.shape[1]
+    name = lax.broadcasted_iota(jnp.int32, (aggs, modes_ref.shape[1]), 0)
+    member = jnp.where(name == agg_ref[...], 1.0, 0.0).astype(jnp.bfloat16)
     sums = {}
 
     def emit(v, i, value):
-        for j in range(6):
-            new_ref[v, i, j] = base_ref[v, i, j] + mask * jnp.broadcast_to(
-                value[j : j + 1, :], (NP, LANES)
-            )
+        lift[pl.ds((v * NP + i) * NP, 6), :] = value
         for a in range(2):
             term = COARSE[a][i] * value
             sums[v, a] = term if i == 0 else sums[v, a] + term
 
     lift_rows(
-        flow_ref, left_ref, own_ref, right_ref, pick, table_ref, jac_ref, work, coef, emit
-    )
+        flow_ref, first_ref, own_ref, second_ref, pick, table_ref, jac_ref, work, coef, emit
+    )
+    fetch.wait()
+    mask = 0.5 * layer_mask()
+    for v in range(NV):
+        for i in range(NP):
+            for j in range(NP):
+                row = (v * NP + i) * NP + j
+                block[v, i, j] += mask * jnp.broadcast_to(lift[row : row + 1, :], (NP, LANES))
+    store = pltpu.make_async_copy(block, new_hbm.at[faces_in], sems.at[1])
+    store.start()
     lane = lax.broadcasted_iota(jnp.int32, (1, LANES), 1)
     jac = jac_ref[:, 0:LANES]
     weight = (0.5 / time_step) / (jac * jac * jac)
     ends = [weight * jnp.where(lane < FACES, COARSE[c][5], COARSE[c][0]) for c in range(2)]
     columns = [column(COARSE[b]) for b in range(2)]
-    rows = []
+    at = lax.broadcasted_iota(jnp.int32, (8, LANES), 0)
+    blocks = []
     for v in range(NV):
+        mode = jnp.zeros((8, LANES), jnp.float32)
         for a in range(2):
             for b in range(2):
                 total = jnp.sum(columns[b] * sums[v, a], axis=0, keepdims=True)
                 for c in range(2):
-                    rows.append(ends[c] * total)
-    count = 8 * NV
-    at = lax.broadcasted_iota(jnp.int32, (8, LANES), 0)
-    blocks = []
-    for v in range(NV):
-        block = jnp.broadcast_to(rows[v * 8], (8, LANES))
-        for r in range(1, 8):
-            block = jnp.where(at == r, rows[v * 8 + r], block)
-        blocks.append(block)
+                    mode = jnp.where(at == a * 4 + b * 2 + c, ends[c] * total, mode)
+        blocks.append(mode)
     faces = modes_ref[:, 0:LANES] + jnp.concatenate(blocks, axis=0)
     modes = jnp.concatenate([faces, modes_ref[:, LANES:]], axis=1)
+    modes = jnp.concatenate(
+        [modes, jnp.zeros((LANES - 8 * NV, modes.shape[1]), jnp.float32)], axis=0
+    )
     high, low = split(modes)
-    aggs = sums_ref.shape[0] * sums_ref.shape[1]
-    name = lax.broadcasted_iota(jnp.int32, (aggs, modes.shape[1]), 0)
-    member = jnp.where(name == agg_ref[...], 1.0, 0.0).astype(jnp.bfloat16)
     contract = (((1,), (1,)), ((), ()))
     total = lax.dot_general(
         member, high, contract, preferred_element_type=jnp.float32
@@ -418,24 +445,40 @@
     share = sums_ref.shape[1]
     for s in range(sums_ref.shape[0]):
         sums_ref[s] = total[s * share : (s + 1) * share, :]
-
-
-def shifted(value, axis, steps):
-    count = lax.axis_size(axis)
-    pairs = [(source, (source + steps) % count) for source in range(count)]
-    return lax.ppermute(value, axis, pairs)
-
-
+    store.wait()
+
+
+def total_kernel(parts_ref, total_ref):
+    total = parts_ref[0]
+    for s in range(1, parts_ref.shape[0]):
+        total = total + parts_ref[s]
+    total_ref[...] = total[:, 0 : total_ref.shape[1]]
+
+
+def swapped(value, first):
+    count = lax.axis_size("blk")
+    edges = [(b, (b + 1) % count) for b in range(first, count, 2)]
+    return lax.ppermute(value, "blk", edges + [(b, a) for a, b in edges])
+
+
+def exchanged(value):
+    late = swapped(value, 0)
+    early = swapped(value, 1)
+    return late, early
+
+
+WHOLE_VMEM = 64800000
 VMEM = pl.BlockSpec(memory_space=pltpu.VMEM)
 SMEM = pl.BlockSpec(memory_space=pltpu.SMEM)
+HBM = pl.BlockSpec(memory_space=pltpu.HBM)
 
 
 def shape(*dims, dtype=jnp.float32):
     return jax.ShapeDtypeStruct(dims, dtype)
 
 
-def params():
-    return pltpu.CompilerParams(vmem_limit_bytes=48 * 1024 * 1024)
+def params(size=48 * 1024 * 1024):
+    return pltpu.CompilerParams(vmem_limit_bytes=size)
 
 
 def local(fields, jacobian, mean_flow, pair_owner, pair_mortar, mortar_proj, coarse_id):
@@ -444,12 +487,10 @@
     aggs = elements * spans // 8
     jac_row = jacobian.reshape(1, elements)
     mats = mortar_proj.reshape(4 * NP * NP)
-    here = jnp.stack([lax.axis_index("blk"), lax.axis_size("blk")]).astype(jnp.int32)
     dims = (NV, NP, NP, NP, LANES)
     half = pl.BlockSpec(dims, lambda n: (0, 0, 0, 0, n))
     row = pl.BlockSpec((1, LANES), lambda n: (0, n))
     whole = pl.BlockSpec((MSG, LANES), lambda n: (0, 0))
-    face_half = pl.BlockSpec(dims, lambda n: (0, 0, 0, 0, 0))
     fixed = lambda *d: pl.BlockSpec(d, lambda n: (0,) * len(d))
     tiles = pltpu.VMEM((NV * NP * NP * 8, LANES), jnp.float32)
     grid = (elements // LANES,)
@@ -459,15 +500,19 @@
 
     message = pl.pallas_call(
         message_kernel,
-        grid=(1,),
-        in_specs=[SMEM, face_half, fixed(1, LANES), fixed(1, LANES)],
-        out_specs=whole,
+        in_specs=[HBM] * 3,
+        out_specs=VMEM,
         out_shape=shape(MSG, LANES),
-        compiler_params=params(),
+        scratch_shapes=[
+            pltpu.VMEM(dims, jnp.float32),
+            pltpu.VMEM((1, LANES), jnp.int32),
+            pltpu.VMEM((1, LANES), jnp.int32),
+            pltpu.SemaphoreType.DMA((3,)),
+        ],
+        compiler_params=params(WHOLE_VMEM),
         name="face_message",
-    )(here, fields, pair_owner.reshape(1, LANES), pair_mortar.reshape(1, LANES))
-    left = shifted(message, "blk", 1)
-    right = shifted(message, "blk", -1)
+    )(fields, pair_owner.reshape(1, LANES), pair_mortar.reshape(1, LANES))
+    first, second = exchanged(message)
 
     rate, trace, table = pl.pallas_call(
         first_volume_kernel,
@@ -496,9 +541,8 @@
         ],
         compiler_params=params(),
         name="first_lift",
-    )(mean_flow, left, message, right, trace, table, jac_row)
-    left2 = shifted(message2, "blk", 1)
-    right2 = shifted(message2, "blk", -1)
+    )(mean_flow, first, message, second, trace, table, jac_row)
+    first2, second2 = exchanged(message2)
 
     base, modes = pl.pallas_call(
         second_volume_kernel,
@@ -514,34 +558,26 @@
 
     new_fields, sums = pl.pallas_call(
         second_lift_kernel,
-        grid=(1,),
-        in_specs=[
-            SMEM,
-            whole,
-            whole,
-            whole,
-            fixed(3 * LANES, 2 * LANES),
-            fixed(144, LANES),
-            fixed(1, elements),
-            fixed(8 * NV, elements),
-            fixed(1, elements),
-            face_half,
-        ],
-        out_specs=[face_half, fixed(spans, aggs // spans, 8 * NV)],
-        out_shape=[shape(*fields.shape), shape(spans, aggs // spans, 8 * NV)],
+        in_specs=[SMEM] + [VMEM] * 8 + [HBM],
+        out_specs=[HBM, VMEM],
+        out_shape=[shape(*fields.shape), shape(spans, aggs // spans, LANES)],
         scratch_shapes=[
             pltpu.VMEM((MSG, 2 * LANES), jnp.float32),
             pltpu.VMEM((36, LANES), jnp.float32),
+            pltpu.VMEM((ROWS, LANES), jnp.float32),
+            pltpu.VMEM(dims, jnp.float32),
+            pltpu.SemaphoreType.DMA((2,)),
         ],
         input_output_aliases={9: 0},
         compiler_params=params(),
         name="second_lift",
     )(
-        mean_flow, left2, message2, right2, pick, table, jac_row, modes,
+        mean_flow, first2, message2, second2, pick, table, jac_row, modes,
         coarse_id.reshape(1, elements), base,
     )
     parts = lax.all_to_all(sums, "span", 0, 0)
-    return new_fields, jnp.sum(parts, axis=0).T
+    coarse = jnp.sum(parts, axis=0)[:, : 8 * NV]
+    return new_fields, coarse.T
 
 
 def solution(mesh):

time: 52.7 us -> 48.7 us (0.924)
  starting transfers between devices: 24.7 us -> 21.4 us
  local copies, waits for them, and re-layouts: 3.57 us -> 0.73 us
  blocking collectives: 10.5 us -> 12.3 us
  other arithmetic: 1.44 us -> 0.01 us
  Pallas kernels: 11.4 us -> 12.5 us
  waiting for transfers between devices: 0.01 us -> 0.61 us
    ppermute x4, starting transfers between devices: 24.7 us -> 21.4 us  [swapped(): return lax.ppermute(value, 'blk', edges + [(b, a) for a, b in edges])]
    unnamed x19 -> x13, local copies, waits for them, and re-layouts: 2.97 us -> 0.03 us
    all_to_all x1, blocking collectives: 10.5 us -> 12.3 us  [local(): parts = lax.all_to_all(sums, 'span', 0, 0)]
    pallas_call x2, Pallas kernels: 3.48 us -> 4.59 us  [the longest x1 2.65 us: local(): pl.pallas_call(second_lift_kernel, in_specs=[SMEM] + [VMEM] * 8 + [HBM],...]
    all_to_all x1 -> x0, other arithmetic: 0.74 us -> none  [local(): parts = lax.all_to_all(sums, 'span', 0, 0)]
    reduce_sum x1, other arithmetic: 0.62 us -> 0.01 us  [local(): coarse = jnp.sum(parts, axis=0)[:, :8 * NV]]
    transpose x0 -> x1, local copies, waits for them, and re-layouts: none -> 0.61 us  [local(): return (new_fields, coarse.T)]
    ppermute x4, waiting for transfers between devices: 0.01 us -> 0.61 us  [swapped(): return lax.ppermute(value, 'blk', edges + [(b, a) for a, b in edges])]
  transfers between devices with their start and end apart: 4 -> 4, of which waited for: 0 -> 1; matrix products, arithmetic and copies ran while one was open for 0% -> 0% of each run, Pallas kernels for 13% -> 14%
where the time goes in v2:
time: 48.7 us; the launch traced here: 48.4 us
  starting transfers between devices  21.4 us (44%)
  Pallas kernels  12.5 us (26%)
  blocking collectives  12.3 us (25%)
  between operations  0.8 us (2%)
  local copies, waits for them, and re-layouts  0.73 us (1%)
  waiting for transfers between devices  0.61 us (1%)
    ppermute x4, starting transfers between devices, swapped(): return lax.ppermute(value, 'blk', edges + [(b, a) for a, b in edges])  21.4 us
    all_to_all x1, blocking collectives, local(): parts = lax.all_to_all(sums, 'span', 0, 0)  12.3 us
    pallas_call x1, Pallas kernels, local(): pl.pallas_call(second_volume_kernel, grid=grid, in_specs=[SMEM, half, row...  3.87 us
    pallas_call x1, Pallas kernels, local(): pl.pallas_call(first_volume_kernel, grid=grid, in_specs=[SMEM, SMEM, half...  2.83 us
    pallas_call x1, Pallas kernels, local(): pl.pallas_call(second_lift_kernel, in_specs=[SMEM] + [VMEM] * 8 + [HBM],...  2.65 us
    pallas_call x1, Pallas kernels, local(): pl.pallas_call(message_kernel, in_specs=[HBM] * 3, out_specs=VMEM, out_sh...  1.94 us
    pallas_call x1, Pallas kernels, local(): pl.pallas_call(first_lift_kernel, in_specs=[SMEM] + [VMEM] * 6, out_specs...  1.21 us
  transfers between devices with their start and end apart: 4, of which 1 were waited for; matrix products, arithmetic and copies ran while one was open for 0% of the time, Pallas kernels for 14%

profile of v2, /device:TPU:1, one launch (start us, length us, event | category | flops | bytes accessed | tf_op | source)
XLA Modules:
  0.0 48.4 jit_solution(17829769990618395330)
XLA Ops:
  0.6 0.0 copy-start
  0.6 0.0 copy-start.5
  0.7 0.0 copy-start.3
  0.7 0.0 copy-start.2
  0.7 1.9 %face_message.1.own_ref = f32[184,128]{1,0:T(8,128)} custom-call(f32[5,6,6,6,256]{4,3,2,1,0:T(8,128)} %fields_ref.3, s32[1,128]{1,0:T(1,128)} %bitcast.11, s32[1,128]{1,0:T(1,128)} %bitcast.12), custom_call_target="tpu_custom_call" | custom-call | tf_op jit(solution)/shard_map/face_message/pallas_call | solution.py:501
  2.6 0.0 copy-start.1
  2.6 14.3 %collective-permute-start.1 = (f32[184,128]{1,0:T(8,128)}, f32[184,128]{1,0:T(8,128)S(1)}, u32[]{:S(2)}, u32[]{:S(2)}) collective-permute-start(f32[184,128]{1,0:T(8,128)} %face_message.1.own_ref), channel_id=1, source_target_pairs={{8,16},{24,32},{40,48},{56,64},{72,80},{88,96},{104,112},{120,128}... | collective-permute-start | bytes 282632 | tf_op jit(solution)/shard_map/ppermute | solution.py:461
  16.9 1.9 %collective-permute-start = (f32[184,128]{1,0:T(8,128)}, f32[184,128]{1,0:T(8,128)S(1)}, u32[]{:S(2)}, u32[]{:S(2)}) collective-permute-start(f32[184,128]{1,0:T(8,128)} %face_message.1.own_ref), channel_id=1, source_target_pairs={{0,8},{16,24},{32,40},{48,56},{64,72},{80,88},{96,104},{112,120},{... | collective-permute-start | bytes 282632 | tf_op jit(solution)/shard_map/ppermute | solution.py:461
  18.8 0.0 copy-done.5
  18.9 0.1 reshape.21.mats_ref
  19.0 0.0 copy-done
  19.0 0.0 copy-done.3
  19.0 0.0 copy-done.2
  19.0 2.8 %first_volume.1 = (f32[5,6,6,6,256]{4,3,2,1,0:T(8,128)S(1)}, f32[184,128]{1,0:T(8,128)S(1)}, f32[144,128]{1,0:T(8,128)S(1)}) custom-call(f32[3]{0:T(128)S(1)} %copy-done.3, f32[144]{0:T(256)S(1)} %reshape.21.mats_ref, f32[5,6,6,6,256]{4,3,2,1,0:T(8,128)S(1)} %copy-done, f32[1,256]{1,0:T(1,128)S(1)} %bitcast.6), custom_call_target="tpu_custom_call" | custom-call | flops 33177600 | bytes 4423680 | tf_op jit(solution)/shard_map/first_volume/pallas_call | solution.py:517
  21.8 0.0 collective-permute-done.1.second_ref
  21.8 0.6 %collective-permute-done.first_ref = f32[184,128]{1,0:T(8,128)S(1)} collective-permute-done((f32[184,128]{1,0:T(8,128)}, f32[184,128]{1,0:T(8,128)S(1)}, u32[]{:S(2)}, u32[]{:S(2)}) %collective-permute-start) | collective-permute-done | bytes 94240 | tf_op jit(solution)/shard_map/ppermute | solution.py:461
  22.4 0.0 copy-done.1
  22.4 1.2 %first_lift.1 = (f32[184,128]{1,0:T(8,128)S(1)}, f32[180,128]{1,0:T(8,128)S(1)}, bf16[384,256]{1,0:T(8,128)(2,1)S(1)}) custom-call(f32[3]{0:T(128)S(1)} %copy-done.3, f32[184,128]{1,0:T(8,128)S(1)} %collective-permute-done.first_ref, f32[184,128]{1,0:T(8,128)S(1)} %copy-done.1, f32[184,128]{1,0:T(8,128)S(1)} %collective-permute-done.1.second_ref, ...), custom_call_target="tpu_custom_call" | custom-call | tf_op jit(solution)/shard_map/first_lift/pallas_call | solution.py:529
  23.7 3.3 %collective-permute-start.3 = (f32[184,128]{1,0:T(8,128)S(1)}, f32[184,128]{1,0:T(8,128)S(1)}, u32[]{:S(2)}, u32[]{:S(2)}) collective-permute-start(f32[184,128]{1,0:T(8,128)S(1)} %get-tuple-element.14.own_ref), channel_id=1, source_target_pairs={{8,16},{24,32},{40,48},{56,64},{72,80},{88,96},{104,112},{120,128}... | collective-permute-start | bytes 282632 | tf_op jit(solution)/shard_map/ppermute | solution.py:461
  27.0 1.9 %collective-permute-start.2 = (f32[184,128]{1,0:T(8,128)S(1)}, f32[184,128]{1,0:T(8,128)S(1)}, u32[]{:S(2)}, u32[]{:S(2)}) collective-permute-start(f32[184,128]{1,0:T(8,128)S(1)} %get-tuple-element.14.own_ref), channel_id=1, source_target_pairs={{0,8},{16,24},{32,40},{48,56},{64,72},{80,88},{96,104},{112,120},{... | collective-permute-start | bytes 282632 | tf_op jit(solution)/shard_map/ppermute | solution.py:461
  28.9 0.0 copy-start.4
  28.9 3.9 %second_volume.1 = (f32[5,6,6,6,256]{4,3,2,1,0:T(8,128)}, f32[40,256]{1,0:T(8,128)S(1)}) custom-call(f32[3]{0:T(128)S(1)} %copy-done.3, f32[5,6,6,6,256]{4,3,2,1,0:T(8,128)S(1)} %copy-done, f32[1,256]{1,0:T(1,128)S(1)} %bitcast.8, f32[5,6,6,6,256]{4,3,2,1,0:T(8,128)S(1)} %get-tuple-element.16.rate_ref, f32[180,128]{1,0:T(8,128)S(1)} %get-tuple-element.17.lift_ref), custom_call_target="tpu_custom_call" | custom-call | flops 33177600 | bytes 4423680 | tf_op jit(solution)/shard_map/second_volume/pallas_call | solution.py:547
  32.8 0.0 collective-permute-done.3.second_ref
  32.8 0.0 collective-permute-done.2.first_ref
  32.8 0.0 copy-done.4
  32.8 2.6 %second_lift.1 = (f32[5,6,6,6,256]{4,3,2,1,0:T(8,128)}, f32[8,32,128]{2,1,0:T(8,128)S(1)}) custom-call(f32[3]{0:T(128)S(1)} %copy-done.3, f32[184,128]{1,0:T(8,128)S(1)} %collective-permute-done.2.first_ref, f32[184,128]{1,0:T(8,128)S(1)} %get-tuple-element.14.own_ref, ...), custom_call_target="tpu_custom_call", output_to_operand_aliasing={{0}: (9, {})} | custom-call | tf_op jit(solution)/shard_map/second_lift/pallas_call | solution.py:559
  35.5 12.3 %all_to_all.5 = f32[8,32,128]{2,1,0:T(8,128)S(1)} all-to-all(f32[8,32,128]{2,1,0:T(8,128)S(1)} %get-tuple-element.21), channel_id=1, replica_groups=mesh['blk'=64,'span'=8] {'span'}, dimensions={0} | all-to-all | bytes 262144 | tf_op jit(solution)/shard_map/all_to_all | solution.py:578
  47.8 0.6 %slice_bitcast_fusion = f32[40,32]{0,1:T(8,128)} fusion(f32[32,128]{1,0:T(8,128)S(1)} %reduce_sum.9), kind=kLoop, calls=%fused_computation | loop fusion | bytes 10240 | tf_op jit(solution)/shard_map/transpose | solution.py:580
  (2 shorter events, 0.0 us)
Async XLA Ops:
  0.6 18.3 %copy-start = (f32[5,6,6,6,256]{4,3,2,1,0:T(8,128)S(1)}, f32[5,6,6,6,256]{4,3,2,1,0:T(8,128)}, u32[]{:S(2)}) copy-start(f32[5,6,6,6,256]{4,3,2,1,0:T(8,128)} %fields_ref.3) | copy-start | bytes 3317764
  0.6 18.2 %copy-start.5 = (f32[2,2,6,6]{3,1,2,0:T(2,128)S(1)}, f32[2,2,6,6]{3,1,2,0:T(2,128)}, u32[]{:S(2)}) copy-start(f32[2,2,6,6]{3,1,2,0:T(2,128)} %param.12) | copy-start | bytes 1732
  0.7 18.3 %copy-start.3 = (f32[3]{0:T(128)S(1)}, f32[3]{0:T(128)}, u32[]{:S(2)}) copy-start(f32[3]{0:T(128)} %flow_ref.7) | copy-start | bytes 40
  0.7 18.3 %copy-start.2 = (f32[256]{0:T(256)S(1)}, f32[256]{0:T(256)}, u32[]{:S(2)}) copy-start(f32[256]{0:T(256)} %param.8) | copy-start | bytes 3076
  2.6 19.8 %copy-start.1 = (f32[184,128]{1,0:T(8,128)S(1)}, f32[184,128]{1,0:T(8,128)}, u32[]{:S(2)}) copy-start(f32[184,128]{1,0:T(8,128)} %face_message.1.own_ref) | copy-start | bytes 282628
  2.6 19.2 %collective-permute-start.1 = (f32[184,128]{1,0:T(8,128)}, f32[184,128]{1,0:T(8,128)S(1)}, u32[]{:S(2)}, u32[]{:S(2)}) collective-permute-start(f32[184,128]{1,0:T(8,128)} %face_message.1.own_ref), channel_id=1, source_target_pairs={{8,16},{24,32},{40,48},{56,64},{72,80},{88,96},{104,112},{120,128}... | collective-permute-start | bytes 282632 | tf_op jit(solution)/shard_map/ppermute | solution.py:461
  16.9 5.5 %collective-permute-start = (f32[184,128]{1,0:T(8,128)}, f32[184,128]{1,0:T(8,128)S(1)}, u32[]{:S(2)}, u32[]{:S(2)}) collective-permute-start(f32[184,128]{1,0:T(8,128)} %face_message.1.own_ref), channel_id=1, source_target_pairs={{0,8},{16,24},{32,40},{48,56},{64,72},{80,88},{96,104},{112,120},{... | collective-permute-start | bytes 282632 | tf_op jit(solution)/shard_map/ppermute | solution.py:461
  23.7 9.1 %collective-permute-start.3 = (f32[184,128]{1,0:T(8,128)S(1)}, f32[184,128]{1,0:T(8,128)S(1)}, u32[]{:S(2)}, u32[]{:S(2)}) collective-permute-start(f32[184,128]{1,0:T(8,128)S(1)} %get-tuple-element.14.own_ref), channel_id=1, source_target_pairs={{8,16},{24,32},{40,48},{56,64},{72,80},{88,96},{104,112},{120,128}... | collective-permute-start | bytes 282632 | tf_op jit(solution)/shard_map/ppermute | solution.py:461
  27.0 5.8 %collective-permute-start.2 = (f32[184,128]{1,0:T(8,128)S(1)}, f32[184,128]{1,0:T(8,128)S(1)}, u32[]{:S(2)}, u32[]{:S(2)}) collective-permute-start(f32[184,128]{1,0:T(8,128)S(1)} %get-tuple-element.14.own_ref), channel_id=1, source_target_pairs={{0,8},{16,24},{32,40},{48,56},{64,72},{80,88},{96,104},{112,120},{... | collective-permute-start | bytes 282632 | tf_op jit(solution)/shard_map/ppermute | solution.py:461
  28.9 3.9 %copy-start.4 = (s32[256]{0:T(256)S(1)}, s32[256]{0:T(256)}, u32[]{:S(2)}) copy-start(s32[256]{0:T(256)} %param.13) | copy-start | bytes 3076
